TPU v7x, 1024 devices: a whole 8x8x8 slice. The times are simulated.
1024 devices in a mesh: cells: 128 (over z, x, core), grp: 8 (over y).
Axes of the slice: x: 8, y: 8, z: 8, core: 2. Of those that a mesh axis runs over, the one named last changes fastest.
Arguments:
- multipoles: bfloat16 [165, 131072], P(None, ('cells', 'grp')), may hold values from -6 to 6
- operators: bfloat16 [165, 165, 128], replicated, may hold values from -0.0625 to 0.0625
- local_pairs: int32 [1024, 16, 2, 256], P(('cells', 'grp')), may hold values from 0 to 127, as said below
- group_pairs: int32 [1024, 8, 2, 256], P(('cells', 'grp')), may hold values from 0 to 127, as said below
- far_pairs: int32 [1024, 8, 2, 256], P(('cells', 'grp')), may hold values from 0 to 127, as said below
- batch_class: int32 [1024, 32], P(('cells', 'grp')), may hold values from 0 to 127
- batch_count: int32 [1024, 32], P(('cells', 'grp')), may hold values from 64 to 256, as said below
- group_send: int32 [128, 8, 8, 8], P('cells'), may hold values from 0 to 127
- far_send: int32 [1024, 128, 1], P(('cells', 'grp')), may hold values from 0 to 127
Outputs:
- local_expansions: float32 [165, 131072], P(None, ('cells', 'grp'))
Inputs may be any that keep to these rules, and one draw needn't show every extreme that they name: `local_pairs`: the two cells of a pair differ. `group_pairs`: entry 0 is a cell of the block, entry 1 a received slot below 64. `far_pairs`: entry 0 is a cell of the block, entry 1 a received slot below 128. `batch_count`: every block has a full batch.
All inputs are finite; a program needn't handle non-finite values.
Results may differ from a plain program's by a relative error of at most 0.0003.
Values may be sent and summed in bfloat16 or wider, within the bound.
No kernel may reach another device: no remote copies, remote signals or barrier semaphores. Data moves between devices by JAX's collectives and lax.ppermute only.
A program may use at most 64 MiB of HBM per device.

v0:
```python
import jax
import jax.numpy as jnp
from jax import lax
from jax.sharding import PartitionSpec as P

ORDER = 8


def degree_signs():
    pieces = [
        jnp.full(((degree + 1) * (degree + 2) // 2,), (-1.0) ** degree, jnp.float32)
        for degree in range(ORDER + 1)
    ]
    return jnp.concatenate(pieces)


def translate_rows(
    op_stack, classes, usable, target_index, source_index, target_table, source_table, start, joined
):
    parity = degree_signs()
    parity_half = parity.astype(jnp.bfloat16)
    zero_value = jnp.zeros((), jnp.bfloat16)
    contract = (((1,), (1,)), ((), ()))

    def step(carry, item):
        klass, keep, target_ids, source_ids = item
        matrix = lax.dynamic_index_in_dim(op_stack, klass, 0, keepdims=False)
        target_rows = jnp.where(
            keep[:, None], jnp.take(target_table, target_ids, axis=0), zero_value
        )
        source_rows = jnp.where(
            keep[:, None], jnp.take(source_table, source_ids, axis=0), zero_value
        )
        to_target = lax.dot_general(
            source_rows, matrix, contract, preferred_element_type=jnp.float32
        )
        flipped = target_rows * parity_half[None, :]
        to_source = parity[None, :] * lax.dot_general(
            flipped, matrix, contract, preferred_element_type=jnp.float32
        )
        if joined:
            return (carry.at[target_ids].add(to_target).at[source_ids].add(to_source), None)
        return (
            (carry[0].at[target_ids].add(to_target), carry[1].at[source_ids].add(to_source)),
            None,
        )

    result, unused = lax.scan(step, start, (classes, usable, target_index, source_index))
    return result


def body(
    multipoles,
    operators,
    local_pairs,
    group_pairs,
    far_pairs,
    batch_class,
    batch_count,
    group_send,
    far_send,
):
    coeff_rows = multipoles.shape[0]
    cell_count = multipoles.shape[1]
    near_list = local_pairs[0]
    group_list = group_pairs[0]
    far_list = far_pairs[0]
    classes = batch_class[0]
    counts = batch_count[0]
    near_batches = near_list.shape[0]
    group_end = near_batches + group_list.shape[0]
    batch_width = near_list.shape[2]
    usable = jnp.arange(batch_width, dtype=jnp.int32)[None, :] < counts[:, None]
    op_stack = jnp.moveaxis(operators, 2, 0)
    own_rows = multipoles.T
    far_cells = far_send[0].reshape(-1)
    far_arrived = lax.all_to_all(
        jnp.take(multipoles, far_cells, axis=1), "cells", split_axis=1, concat_axis=1, tiled=True
    )
    start = jnp.zeros((cell_count, coeff_rows), jnp.float32)
    totals = translate_rows(
        op_stack,
        classes[:near_batches],
        usable[:near_batches],
        near_list[:, 0],
        near_list[:, 1],
        own_rows,
        own_rows,
        start,
        True,
    )
    group_rank = lax.axis_index("grp")
    group_size = lax.axis_size("grp")
    group_classes = classes[near_batches:group_end]
    group_usable = usable[near_batches:group_end]
    send_table = lax.dynamic_index_in_dim(group_send[0], group_rank, 1, keepdims=False)
    column_map = (
        jnp.arange(group_size, dtype=jnp.int32)[:, None] * cell_count + send_table
    ).reshape(-1)
    source_index = jnp.take(column_map, group_list[:, 1], axis=0)
    everyone = lax.all_gather(multipoles, "grp", axis=1, tiled=True)
    spread_start = jnp.zeros((everyone.shape[1], coeff_rows), jnp.float32)
    totals, spread = translate_rows(
        op_stack,
        group_classes,
        group_usable,
        group_list[:, 0],
        source_index,
        own_rows,
        everyone.T,
        (totals, spread_start),
        False,
    )
    totals = totals + lax.psum_scatter(spread.T, "grp", scatter_dimension=1, tiled=True).T
    far_start = jnp.zeros((far_arrived.shape[1], coeff_rows), jnp.float32)
    totals, far_back = translate_rows(
        op_stack,
        classes[group_end:],
        usable[group_end:],
        far_list[:, 0],
        far_list[:, 1],
        own_rows,
        far_arrived.T,
        (totals, far_start),
        False,
    )
    far_home = lax.all_to_all(far_back.T, "cells", split_axis=1, concat_axis=1, tiled=True)
    totals = totals.at[far_cells].add(far_home.T)
    return totals.T


def solution(mesh):
    placed = (
        P(None, ("cells", "grp")),
        P(),
        P(("cells", "grp"), None, None, None),
        P(("cells", "grp"), None, None, None),
        P(("cells", "grp"), None, None, None),
        P(("cells", "grp"), None),
        P(("cells", "grp"), None),
        P("cells", None, None, None),
        P(("cells", "grp"), None, None),
    )
    return jax.shard_map(
        body, mesh=mesh, in_specs=placed, out_specs=P(None, ("cells", "grp")), check_vma=False
    )
```

profile of v0, /device:TPU:1, one launch (start us, length us, event | category | flops | bytes accessed | tf_op | source)
XLA Modules:
  0.0 519.9 jit_solution(17865154564395730622)
XLA Ops:
  11.2 15.2 %copy.55 = bf16[165,165,128]{1,0,2:T(8,128)(2,1)} copy(bf16[165,165,128]{2,1,0:T(8,128)(2,1)} %param.18) | data formatting | bytes 13939200 | tf_op args[1]
  26.4 21.9 %all_gather.3 = bf16[165,1024]{0,1:T(8,128)(2,1)S(1)} all-gather(bf16[165,128]{0,1:T(8,128)(2,1)S(1)} %copy.54), channel_id=1, replica_groups=mesh['cells'=128,'grp'=8] {'grp'}, dimensions={1}, use_global_device_ids=true | all-gather | bytes 380160 | tf_op jit(solution)/shard_map/all_gather | solution.py:101
  48.4 179.0 %while.34 = (s32[]{:T(128)}, f32[128,165]{1,0:T(8,128)S(1)}, s32[16,256]{1,0:T(8,128)S(1)}, pred[16,256]{1,0:T(8,128)(4,1)S(1)}, s32[16,256]{1,0:T(8,128)S(1)}, ...) while((s32[]{:T(128)}, f32[128,165]{1,0:T(8,128)S(1)}, ...), condition=%wide.region_3.5_spmd, body=%wide.region_0.4_spmd.sunk | while | flops 28224516 | bytes 2398369 | solution.py:48
  57.5 2.0 scatter_fusion.1
  68.7 2.0 scatter_fusion.1
  79.9 2.0 scatter_fusion.1
  91.1 2.0 scatter_fusion.1
  102.3 2.0 scatter_fusion.1
  113.5 2.0 scatter_fusion.1
  124.7 2.0 scatter_fusion.1
  135.8 2.0 scatter_fusion.1
  147.0 2.0 scatter_fusion.1
  158.2 2.0 scatter_fusion.1
  169.4 2.0 scatter_fusion.1
  180.6 2.0 scatter_fusion.1
  191.8 2.0 scatter_fusion.1
  227.7 12.6 %gather_fusion.6 = s32[2048]{0:T(1024)S(1)} fusion(s32[64]{0:T(128)S(1)} %add.180, s32[2048]{0:T(1024)S(1)} %broadcast_clamp_fusion), kind=kCustom, calls=%fused_computation.6 | custom fusion | bytes 24576 | tf_op jit(solution)/shard_map/jit(_take)/gather | solution.py:100
  240.5 91.9 %while.35 = (s32[]{:T(128)}, f32[128,165]{1,0:T(8,128)S(1)}, f32[1024,165]{1,0:T(8,128)S(1)}, s32[8,256]{1,0:T(8,128)S(1)}, pred[8,256]{1,0:T(8,128)(4,1)S(1)}, ...) while((s32[]{:T(128)}, f32[128,165]{1,0:T(8,128)S(1)}, ...), condition=%wide.region_7.9_spmd, body=%wide.region_4.8_spmd.sunk | while | flops 28223748 | bytes 2396337 | solution.py:48
  249.6 2.4 scatter_fusion.3
  261.1 2.4 scatter_fusion.3
  272.6 2.4 scatter_fusion.3
  284.1 2.4 scatter_fusion.3
  295.6 2.4 scatter_fusion.3
  307.1 2.4 scatter_fusion.3
  318.5 2.4 scatter_fusion.3
  330.0 2.4 scatter_fusion.3
  335.2 30.3 %all-to-all-start = ((bf16[165,128,1]{0,2,1:T(2,128)(2,1)}), bf16[165,128,1]{0,2,1:T(2,128)(2,1)S(1)}, u32[]{:S(2)}, u32[]{:S(2)}) async-start(bf16[165,128,1]{0,2,1:T(2,128)(2,1)} %copy.60), calls=%async_computation.1 | async-start | bytes 262144 | tf_op jit(solution)/shard_map/all_to_all | solution.py:77
  365.5 12.6 %all-to-all-done = bf16[165,128,1]{0,2,1:T(2,128)(2,1)S(1)} async-done(((bf16[165,128,1]{0,2,1:T(2,128)(2,1)}), bf16[165,128,1]{0,2,1:T(2,128)(2,1)S(1)}, u32[]{:S(2)}, u32[]{:S(2)}) %all-to-all-start) | async-done | bytes 42272 | tf_op jit(solution)/shard_map/all_to_all | solution.py:77
  378.1 10.1 %reduce-scatter.2.cloned.1.call-done = f32[165,128]{0,1:T(8,128)} async-done(((f32[165,1024]{0,1:T(8,128)}), f32[165,128]{0,1:T(8,128)}) %reduce-scatter.2.cloned.1.call-update) | async-done | bytes 84496 | tf_op jit(solution)/shard_map/reduce_scatter | solution.py:114
  389.1 89.5 %while.36 = (s32[]{:T(128)}, f32[128,165]{1,0:T(8,128)S(1)}, f32[128,165]{1,0:T(8,128)S(1)}, s32[8,256]{1,0:T(8,128)S(1)}, pred[8,256]{1,0:T(8,128)(4,1)S(1)}, /...) while((s32[]{:T(128)}, f32[128,165]{1,0:T(8,128)S(1)}, ...), condition=%wide.region_12.14_spmd, body=%wide.region_9.13_spmd.sunk | while | flops 28224516 | bytes 2398385 | solution.py:48
  409.5 2.0 scatter_fusion.5
  478.8 32.1 %all_to_all.21 = f32[165,128,1]{0,2,1:T(1,128)S(1)} all-to-all(f32[165,128,1]{0,2,1:T(1,128)S(1)} %copy.64), channel_id=1, replica_groups=mesh['cells'=128,'grp'=8] {'cells'}, dimensions={1} | all-to-all | bytes 168960 | tf_op jit(solution)/shard_map/all_to_all | solution.py:127
  (534 shorter events, 268.7 us)
Async XLA Ops:
  6.5 221.0 %copy-start = (s32[1,8,8,8]{3,2,1,0:T(8,128)S(1)}, s32[1,8,8,8]{3,2,1,0:T(8,128)}, u32[]{:S(2)}) copy-start(s32[1,8,8,8]{3,2,1,0:T(8,128)} %param.24) | copy-start | bytes 6148
  6.5 41.8 %copy-start.4 = (f32[165]{0:T(256)S(1)}, f32[165]{0:T(256)}, u32[]{:S(2)}) copy-start(f32[165]{0:T(256)} %constant.84.clone.1) | copy-start | bytes 1984
  6.5 41.8 %copy-start.5 = (bf16[165]{0:T(256)(128)(2,1)S(1)}, bf16[165]{0:T(256)(128)(2,1)}, u32[]{:S(2)}) copy-start(bf16[165]{0:T(256)(128)(2,1)} %constant.85.clone.1) | copy-start | bytes 994
  6.5 381.7 %reduce-scatter.2.cloned.1.call-start = ((), (), s32[]{:S(2)}) async-start(), calls=%async_computation.3 | async-start | bytes 1179648 | tf_op jit(solution)/shard_map/reduce_scatter | solution.py:114
  240.4 93.0 %copy-start.3 = (s32[1,128,1]{1,2,0:T(1,128)S(1)}, s32[1,128,1]{1,2,0:T(1,128)}, u32[]{:S(2)}) copy-start(s32[1,128,1]{1,2,0:T(1,128)} %param.25) | copy-start | bytes 1540
  240.4 125.0 %copy-start.2 = (s32[1,8,2,256]{3,2,1,0:T(2,128)S(1)}, s32[1,8,2,256]{3,2,1,0:T(2,128)}, u32[]{:S(2)}) copy-start(s32[1,8,2,256]{3,2,1,0:T(2,128)} %param.21) | copy-start | bytes 49156
  332.4 1.0 copy-start.1
  335.2 43.0 %all-to-all-start = ((bf16[165,128,1]{0,2,1:T(2,128)(2,1)}), bf16[165,128,1]{0,2,1:T(2,128)(2,1)S(1)}, u32[]{:S(2)}, u32[]{:S(2)}) async-start(bf16[165,128,1]{0,2,1:T(2,128)(2,1)} %copy.60), calls=%async_computation.1 | async-start | bytes 262144 | tf_op jit(solution)/shard_map/all_to_all | solution.py:77
Sparse Core Ops, SparseCore 0:
  333.5 54.6 reduce-scatter.1
where the time goes:
time: 524 us; the launch traced here: 520 us
  other arithmetic  137 us (26%)
  local copies, waits for them, and re-layouts  132 us (25%)
  matrix products  74.5 us (14%)
  loops' own time  55.2 us (11%)
  blocking collectives  54.1 us (10%)
  starting transfers between devices  30.3 us (6%)
  waiting for transfers between devices  22.7 us (4%)
  between operations  13.7 us (3%)
    scatter-add x32, other arithmetic, step(): carry.at[target_ids].add(to_target).at[source_ids].add(to_source)  65 us
    another operation x3, loops' own time, translate_rows(): lax.scan(step, start, (classes, usable, target_index, source_index))  55.2 us
    dot_general x32, matrix products, step(): lax.dot_general(flipped, matrix, contract, preferred_element_type=jnp.flo...  37.9 us
    gather x32, local copies, waits for them, and re-layouts, step(): jnp.take(source_table, source_ids, axis=0)  36.9 us
    gather x32, local copies, waits for them, and re-layouts, step(): jnp.take(target_table, target_ids, axis=0)  36.9 us
    dot_general x32, matrix products, step(): lax.dot_general(source_rows, matrix, contract, preferred_element_type=jnp...  36.7 us
    scatter-add x16, other arithmetic, step(): carry[1].at[source_ids].add(to_source)  35.2 us
    scatter-add x16, other arithmetic, step(): carry[0].at[target_ids].add(to_target)  32.5 us
  transfers between devices with their start and end apart: 2, of which 2 were waited for; matrix products, arithmetic and copies ran while one was open for 0% of the time, Pallas kernels for 0%

commit v1 on v0

v1 whole, which is shorter than its diff:
```python
import functools

import jax
import jax.numpy as jnp
import numpy as np
from jax import lax
from jax.experimental import pallas as pl
from jax.experimental.pallas import tpu as pltpu
from jax.sharding import PartitionSpec as P

ORDER = 8
LANES = 128
WIDE = 256
PAD_ROWS = 176
STEP_ROWS = 15
BF = jnp.bfloat16
F32 = jnp.float32
VMEM_LIMIT = 56 * 1024 * 1024


def degree_signs():
    return np.concatenate(
        [np.full(((d + 1) * (d + 2) // 2,), (-1.0) ** d, np.float32) for d in range(ORDER + 1)]
    )


def lane_signs():
    signs = np.zeros((1, WIDE), np.float32)
    signs[0, : degree_signs().size] = degree_signs()
    return signs


def dot_nt(a, b):
    return lax.dot_general(a, b, (((1,), (1,)), ((), ())), preferred_element_type=F32)


def dot_nn(a, b):
    return lax.dot_general(a, b, (((1,), (0,)), ((), ())), preferred_element_type=F32)


def split(x):
    high = x.astype(BF)
    low = (x - high.astype(F32)).astype(BF)
    return high, low


def one_hot(ids, size):
    rows = lax.broadcasted_iota(jnp.int32, (size, ids.shape[1]), 0)
    return jnp.where(rows == ids, 1.0, 0.0).astype(BF)


def pair_hots(pairs_ref, batch, count, first, second):
    targets = pairs_ref[0, batch, 0:1, :]
    sources = pairs_ref[0, batch, 1:2, :]
    spots = lax.broadcasted_iota(jnp.int32, targets.shape, 1)
    targets = jnp.where(spots < count, targets, -1)
    return one_hot(targets, first), one_hot(sources, second)


def padded_rows(own):
    own = own.astype(F32)
    return jnp.concatenate([own, jnp.zeros((WIDE - own.shape[0], own.shape[1]), F32)], axis=0)


def scalar_row(read, count):
    lanes = lax.broadcasted_iota(jnp.int32, (1, LANES), 1)
    row = jnp.full((1, LANES), -1, jnp.int32)
    for i in range(count):
        row = jnp.where(lanes == i, read(i), row)
    return row


def prepare_kernel(
    batch_class, batch_count, me, group_send, own_ref, ops_ref, group_ref, far_ref, far_send_ref,
    signs_ref, far_out, group_out, near_ops, rest_ops, hot_class, low_table, high_table,
):
    step = pl.program_id(0)
    batches = batch_class.shape[1]
    coeffs = own_ref.shape[0]
    cells = own_ref.shape[1]
    near = near_ops.shape[0]
    group_batches = group_ref.shape[1]
    far_batches = far_ref.shape[1]
    group_slots = group_out.shape[0]
    far_slots = far_out.shape[0] // 4

    @pl.when(step == 0)
    def _():
        rows = lax.broadcasted_iota(jnp.int32, (batches, LANES), 0)
        lanes = lax.broadcasted_iota(jnp.int32, (batches, LANES), 1)
        wanted = jnp.zeros((batches, LANES), jnp.int32)
        for i in range(batches):
            wanted = jnp.where(rows == i, batch_class[0, i], wanted)
        hot_class[...] = jnp.where(lanes == wanted, 1.0, 0.0).astype(BF)
        high_table[...] = jnp.zeros(high_table.shape, F32)
        low_table[coeffs * batches :, :] = jnp.zeros(((PAD_ROWS - coeffs) * batches, LANES), F32)

    hot = hot_class[...]
    for i in range(STEP_ROWS):
        picked = dot_nt(hot, ops_ref[i])
        start = pl.multiple_of((step * STEP_ROWS + i) * batches, batches)
        low_table[pl.ds(start, batches), :] = picked[:, :LANES]
        high_table[pl.ds(start, batches), : coeffs - LANES] = picked[:, LANES:]

    @pl.when(step == pl.num_programs(0) - 1)
    def _():
        def matrix(i):
            low = low_table[pl.ds(i, PAD_ROWS, stride=batches), :]
            high = high_table[pl.ds(i, PAD_ROWS, stride=batches), :]
            return jnp.concatenate([low, high], axis=1).astype(BF)

        signs = signs_ref[...]
        own = padded_rows(own_ref[...])
        own_half = own.astype(BF)
        sign_column = jnp.transpose(jnp.broadcast_to(signs, (LANES, WIDE)))
        flipped = (own * sign_column[:, :cells]).astype(BF)

        def back_terms(pairs_ref, count_batches, first_batch, slots):
            counts = []
            for b in range(count_batches):
                hot_t, hot_u = pair_hots(
                    pairs_ref, b, batch_count[0, first_batch + b], cells, slots
                )
                counts.append(dot_nt(hot_u, hot_t).astype(BF))
            summed = dot_nt(jnp.concatenate(counts, axis=0), flipped)
            total = jnp.zeros((slots, PAD_ROWS), F32)
            for b in range(count_batches):
                high, low = split(summed[b * slots : (b + 1) * slots])
                both = dot_nt(jnp.concatenate([high, low], axis=0), matrix(first_batch + b))
                total = total + both[:slots] + both[slots:]
            return total * signs[:, :PAD_ROWS]

        far_back = back_terms(far_ref, far_batches, near + group_batches, far_slots)
        far_hot = one_hot(far_send_ref[...], cells)
        far_own = jnp.transpose(dot_nn(own_half, far_hot))
        far_out[pl.ds(0, far_slots, stride=4), :] = far_back[:, :LANES]
        far_out[pl.ds(1, far_slots, stride=4), :] = jnp.concatenate(
            [far_back[:, LANES:], jnp.zeros((far_slots, WIDE - PAD_ROWS), F32)], axis=1
        )
        far_out[pl.ds(2, far_slots, stride=4), :] = far_own[:, :LANES]
        far_out[pl.ds(3, far_slots, stride=4), :] = far_own[:, LANES:]

        group_back = back_terms(group_ref, group_batches, near, group_slots)
        row = scalar_row(lambda i: group_send[0, me[0], i // 8, i % 8], group_slots)
        group_hot = one_hot(row, cells)
        group_own = jnp.transpose(dot_nn(own_half, group_hot))[:group_slots]
        group_out[:, :LANES] = group_back[:, :LANES]
        group_out[:, LANES:WIDE] = jnp.concatenate(
            [group_back[:, LANES:], jnp.zeros((group_slots, WIDE - PAD_ROWS), F32)], axis=1
        )
        group_out[:, WIDE:] = group_own
        for i in range(near):
            near_ops[i] = matrix(i)
        for i in range(batches - near):
            rest_ops[i] = matrix(near + i)


def near_kernel(batch_count, own_ref, near_ref, ops_ref, signs_ref, out_ref):
    cells = own_ref.shape[1]
    near = ops_ref.shape[0]
    signs = signs_ref[...]
    own = padded_rows(own_ref[...])
    own_half = own.astype(BF)
    sign_column = jnp.transpose(jnp.broadcast_to(signs, (LANES, WIDE)))
    flipped = (own * sign_column[:, :cells]).astype(BF)
    forward, backward = [], []
    for b in range(near):
        hot_t, hot_u = pair_hots(near_ref, b, batch_count[0, b], cells, cells)
        forward.append(dot_nt(hot_t, hot_u).astype(BF))
        backward.append(dot_nt(hot_u, hot_t).astype(BF))
    ahead = dot_nt(jnp.concatenate(forward, axis=0), own_half)
    behind = dot_nt(jnp.concatenate(backward, axis=0), flipped)
    total = jnp.zeros((cells, PAD_ROWS), F32)
    mirrored = jnp.zeros((cells, PAD_ROWS), F32)
    for b in range(near):
        part = slice(b * cells, (b + 1) * cells)
        both = dot_nt(
            jnp.concatenate([*split(ahead[part]), *split(behind[part])], axis=0), ops_ref[b]
        )
        total = total + both[:cells] + both[cells : 2 * cells]
        mirrored = mirrored + both[2 * cells : 3 * cells] + both[3 * cells :]
    out_ref[...] = total + mirrored * signs[:, :PAD_ROWS]


def finish_kernel(
    batch_count, me, group_send, near_sum, ops_ref, group_ref, far_ref, far_send_ref, far_in,
    group_in, out_ref,
):
    cells = out_ref.shape[1]
    coeffs = out_ref.shape[0]
    group_batches = group_ref.shape[1]
    far_batches = far_ref.shape[1]
    near = batch_count.shape[1] - group_batches - far_batches
    far_slots = far_in.shape[0] // 4
    group_slots = group_in.shape[0]
    total = near_sum[...]

    def forward_terms(pairs_ref, count_batches, first_batch, slots, arrived, total):
        counts = []
        for b in range(count_batches):
            hot_t, hot_u = pair_hots(pairs_ref, b, batch_count[0, near + first_batch + b], cells, slots)
            counts.append(dot_nt(hot_t, hot_u).astype(BF))
        summed = dot_nn(jnp.concatenate(counts, axis=0), arrived)
        for b in range(count_batches):
            high, low = split(summed[b * cells : (b + 1) * cells])
            both = dot_nt(jnp.concatenate([high, low], axis=0), ops_ref[first_batch + b])
            total = total + both[:cells] + both[cells:]
        return total

    def piece(i):
        return far_in[pl.ds(i, far_slots, stride=4), :]

    far_arrived = jnp.concatenate([piece(2), piece(3)], axis=1).astype(BF)
    total = forward_terms(far_ref, far_batches, group_batches, far_slots, far_arrived, total)
    group_arrived = group_in[:, WIDE:].astype(BF)
    total = forward_terms(group_ref, group_batches, 0, group_slots, group_arrived, total)

    far_hot = one_hot(far_send_ref[...], cells)
    home_high, home_low = split(jnp.concatenate([piece(0), piece(1)], axis=1))
    row = scalar_row(lambda i: group_send[0, me[0], i // 8, i % 8], group_slots)
    group_hot = one_hot(row, cells)[:, :group_slots]
    back_high, back_low = split(group_in[:, :WIDE])
    home = dot_nn(far_hot, home_high) + dot_nn(far_hot, home_low)
    home = home + dot_nn(group_hot, back_high) + dot_nn(group_hot, back_low)
    total = total + home[:, :PAD_ROWS]
    total = jnp.concatenate([total, jnp.zeros((cells, WIDE - PAD_ROWS), F32)], axis=1)
    out_ref[...] = jnp.transpose(total)[:coeffs]


def body(
    multipoles, operators, local_pairs, group_pairs, far_pairs, batch_class, batch_count,
    group_send, far_send,
):
    coeffs, cells = multipoles.shape
    batches = batch_class.shape[1]
    near = local_pairs.shape[1]
    group_size = lax.axis_size("grp")
    ranges = lax.axis_size("cells")
    far_slots = far_send.shape[1] * far_send.shape[2]
    far_send = far_send.reshape(1, far_slots)
    group_slots = group_size * group_send.shape[3]
    me = lax.axis_index("grp").reshape(1)
    signs = jnp.asarray(lane_signs())
    smem = pl.BlockSpec(memory_space=pltpu.SMEM)
    vmem = pl.BlockSpec(memory_space=pltpu.VMEM)
    params = pltpu.CompilerParams(vmem_limit_bytes=VMEM_LIMIT)

    def whole(a):
        zeros = (0,) * a.ndim
        return pl.BlockSpec(a.shape, lambda i: zeros)

    def out_block(shape):
        zeros = (0,) * len(shape)
        return pl.BlockSpec(shape, lambda i: zeros)

    shapes = [
        jax.ShapeDtypeStruct((far_slots * 4, LANES), F32),
        jax.ShapeDtypeStruct((group_slots, 2 * WIDE), F32),
    ]
    far_rows, group_rows, ops_near, ops_rest = pl.pallas_call(
        prepare_kernel,
        grid=(coeffs // STEP_ROWS,),
        in_specs=[smem] * 4
        + [
            whole(multipoles),
            pl.BlockSpec((STEP_ROWS,) + operators.shape[1:], lambda i: (i, 0, 0)),
            whole(group_pairs),
            whole(far_pairs),
            whole(far_send),
            whole(signs),
        ],
        out_shape=shapes
        + [
            jax.ShapeDtypeStruct((near, PAD_ROWS, WIDE), BF),
            jax.ShapeDtypeStruct((batches - near, PAD_ROWS, WIDE), BF),
        ],
        out_specs=[
            out_block(shapes[0].shape),
            out_block(shapes[1].shape),
            out_block((near, PAD_ROWS, WIDE)),
            out_block((batches - near, PAD_ROWS, WIDE)),
        ],
        scratch_shapes=[
            pltpu.VMEM((batches, LANES), BF),
            pltpu.VMEM((PAD_ROWS * batches, LANES), F32),
            pltpu.VMEM((PAD_ROWS * batches, LANES), F32),
        ],
        compiler_params=params,
        name="prepare",
    )(
        batch_class, batch_count, me, group_send, multipoles, operators, group_pairs, far_pairs,
        far_send, signs,
    )
    far_got = lax.all_to_all(
        far_rows.reshape(ranges, -1, LANES), "cells", split_axis=0, concat_axis=0, tiled=True
    ).reshape(far_rows.shape)
    group_got = lax.all_to_all(
        group_rows.reshape(group_size, -1, 2 * WIDE), "grp", split_axis=0, concat_axis=0, tiled=True
    ).reshape(group_rows.shape)
    near_sum = pl.pallas_call(
        near_kernel,
        in_specs=[smem] + [vmem] * 4,
        out_specs=vmem,
        out_shape=jax.ShapeDtypeStruct((cells, PAD_ROWS), F32),
        compiler_params=params,
        cost_estimate=pl.CostEstimate(
            flops=20_000_000_000, bytes_accessed=40_000_000, transcendentals=0
        ),
        name="near",
    )(batch_count, multipoles, local_pairs, ops_near, signs)
    return pl.pallas_call(
        finish_kernel,
        in_specs=[smem] * 3 + [vmem] * 7,
        out_specs=vmem,
        out_shape=jax.ShapeDtypeStruct((coeffs, cells), F32),
        compiler_params=params,
        name="finish",
    )(
        batch_count, me, group_send, near_sum, ops_rest, group_pairs, far_pairs, far_send, far_got,
        group_got,
    )


def solution(mesh):
    placed = (
        P(None, ("cells", "grp")),
        P(),
        P(("cells", "grp"), None, None, None),
        P(("cells", "grp"), None, None, None),
        P(("cells", "grp"), None, None, None),
        P(("cells", "grp"), None),
        P(("cells", "grp"), None),
        P("cells", None, None, None),
        P(("cells", "grp"), None, None),
    )
    return jax.shard_map(
        body, mesh=mesh, in_specs=placed, out_specs=P(None, ("cells", "grp")), check_vma=False
    )
```

time: 524 us -> 82.7 us (0.16)
  other arithmetic: 137 us -> 0 us
  local copies, waits for them, and re-layouts: 132 us -> 0.69 us
  matrix products: 74.5 us -> 0 us
  loops' own time: 55.2 us -> 0 us
  blocking collectives: 54.1 us -> 16.1 us
  Pallas kernels: 0 us -> 30.2 us
  between operations: 13.7 us -> 0.01 us
  waiting for transfers between devices: 22.7 us -> 10 us
    scatter-add x65 -> x0, other arithmetic: 134 us -> none  [the longest x32 65 us: step(): carry.at[target_ids].add(to_target).at[source_ids].add(to_source)]
    gather x67 -> x0, local copies, waits for them, and re-layouts: 87.2 us -> none  [the longest x32 36.9 us: step(): jnp.take(source_table, source_ids, axis=0)]
    dot_general x64 -> x0, matrix products: 74.5 us -> none  [the longest x32 37.9 us: step(): lax.dot_general(flipped, matrix, contract, preferred_element_type=jnp.flo...]
    another operation x3 -> x0, loops' own time: 55.2 us -> none  [translate_rows(): lax.scan(step, start, (classes, usable, target_index, source_index))]
    pallas_call x0 -> x3, Pallas kernels: none -> 30.2 us  [the longest x1 21 us: body(): pl.pallas_call(prepare_kernel, grid=(coeffs // STEP_ROWS,), in_specs=[sme...]
    all_gather x1 -> x0, blocking collectives: 21.9 us -> none  [body(): everyone = lax.all_gather(multipoles, 'grp', axis=1, tiled=True)]
    dynamic_slice x65 -> x0, local copies, waits for them, and re-layouts: 18.6 us -> none  [the longest x64 18.6 us: translate_rows(): lax.scan(step, start, (classes, usable, target_index, source_index))]
    unnamed x18 -> x2, local copies, waits for them, and re-layouts: 18.6 us -> 0.69 us
  transfers between devices with their start and end apart: 2 -> 1, of which waited for: 2 -> 1; matrix products, arithmetic and copies ran while one was open for 0% -> 0% of each run, Pallas kernels for 0% -> 6%
where the time goes in v1:
time: 82.7 us; the launch traced here: 82.2 us
  Pallas kernels  30.2 us (37%)
  starting transfers between devices  25.1 us (30%)
  blocking collectives  16.1 us (19%)
  waiting for transfers between devices  10 us (12%)
    all_to_all x1, starting transfers between devices, body(): lax.all_to_all(far_rows.reshape(ranges, -1, LANES), 'cells', split_axis=0...  25.1 us
    pallas_call x1, Pallas kernels, body(): pl.pallas_call(prepare_kernel, grid=(coeffs // STEP_ROWS,), in_specs=[sme...  21 us
    all_to_all x1, blocking collectives, body(): lax.all_to_all(group_rows.reshape(group_size, -1, 2 * WIDE), 'grp', split...  16.1 us
    all_to_all x1, waiting for transfers between devices, body(): lax.all_to_all(far_rows.reshape(ranges, -1, LANES), 'cells', split_axis=0...  10 us
    pallas_call x1, Pallas kernels, body(): pl.pallas_call(near_kernel, in_specs=[smem] + [vmem] * 4, out_specs=vmem,...  5.2 us
    pallas_call x1, Pallas kernels, body(): pl.pallas_call(finish_kernel, in_specs=[smem] * 3 + [vmem] * 7, out_specs...  4.07 us
  transfers between devices with their start and end apart: 1, of which 1 were waited for; matrix products, arithmetic and copies ran while one was open for 0% of the time, Pallas kernels for 6%

profile of v1, /device:TPU:1, one launch (start us, length us, event | category | flops | bytes accessed | tf_op | source)
XLA Modules:
  0.0 82.2 jit_solution(10179851205952065380)
XLA Ops:
  0.0 21.0 %prepare.1 = (f32[512,128]{1,0:T(8,128)}, f32[64,512]{1,0:T(8,128)}, bf16[16,176,256]{2,1,0:T(8,128)(2,1)}, bf16[16,176,256]{2,1,0:T(8,128)(2,1)}) custom-call(s32[1,32]{1,0:T(1,128)} %batch_class.1, s32[1,32]{1,0:T(1,128)} %batch_count.5, s32[1]{0:T(128)} %bitcast.me, s32[1,8,8,8]{3,2,1,0:T(8,128)} %group_send.3, bf16[165,128]{1,0:T(8,128)(2,1)} %own_ref.3, ...), custom_call_target="tpu_custom_call" | custom-call | tf_op jit(solution)/shard_map/prepare/pallas_call | solution.py:260
  21.0 16.1 %all_to_all.10 = f32[8,8,512]{2,1,0:T(8,128)} all-to-all(f32[8,8,512]{2,1,0:T(8,128)} %bitcast.9), channel_id=1, replica_groups=mesh['cells'=128,'grp'=8] {'grp'}, dimensions={0} | all-to-all | bytes 262144 | tf_op jit(solution)/shard_map/all_to_all | solution.py:297
  37.1 25.1 %all-to-all-start = ((f32[128,4,128]{2,1,0:T(4,128)}), f32[128,4,128]{2,1,0:T(4,128)S(1)}, u32[]{:S(2)}, u32[]{:S(2)}) async-start(f32[128,4,128]{2,1,0:T(4,128)} %bitcast.8), calls=%async_computation | async-start | bytes 524288 | tf_op jit(solution)/shard_map/all_to_all | solution.py:294
  62.2 5.2 %near.1.near_sum = f32[128,176]{1,0:T(8,128)} custom-call(s32[1,32]{1,0:T(1,128)} %batch_count.5, bf16[165,128]{1,0:T(8,128)(2,1)} %own_ref.3, s32[1,16,2,256]{3,2,1,0:T(2,128)} %near_ref.1, bf16[16,176,256]{2,1,0:T(8,128)(2,1)} %get-tuple-element.9.ops_ref, f32[1,256]{1,0:T(1,128)} %constant.6.clone.signs_ref), custom_call_target="tpu_custom_call" | custom-call | flops 20000000000 | bytes 40000000 | tf_op jit(solution)/shard_map/near/pallas_call | solution.py:300
  67.4 10.0 %all-to-all-done = f32[128,4,128]{2,1,0:T(4,128)S(1)} async-done(((f32[128,4,128]{2,1,0:T(4,128)}), f32[128,4,128]{2,1,0:T(4,128)S(1)}, u32[]{:S(2)}, u32[]{:S(2)}) %all-to-all-start) | async-done | bytes 262176 | tf_op jit(solution)/shard_map/all_to_all | solution.py:294
  77.4 0.0 copy-start
  77.4 0.7 copy-done
  78.1 4.1 %finish.1 = f32[165,128]{1,0:T(8,128)} custom-call(s32[1,32]{1,0:T(1,128)} %batch_count.5, s32[1]{0:T(128)} %bitcast.me, s32[1,8,8,8]{3,2,1,0:T(8,128)} %group_send.3, f32[128,176]{1,0:T(8,128)} %near.1.near_sum, bf16[16,176,256]{2,1,0:T(8,128)(2,1)} %get-tuple-element.10.ops_ref, s32[1,8,2,256]{3,2,1,0:T(2,128)} %group_ref.3, s32[1,8,2,256]{3,2,1,0:T(2,128)} %far_ref.3, ...), custom_call_target="tpu_custom_call" | custom-call | tf_op jit(solution)/shard_map/finish/pallas_call | solution.py:311
Async XLA Ops:
  37.1 40.3 %all-to-all-start = ((f32[128,4,128]{2,1,0:T(4,128)}), f32[128,4,128]{2,1,0:T(4,128)S(1)}, u32[]{:S(2)}, u32[]{:S(2)}) async-start(f32[128,4,128]{2,1,0:T(4,128)} %bitcast.8), calls=%async_computation | async-start | bytes 524288 | tf_op jit(solution)/shard_map/all_to_all | solution.py:294
  77.4 0.7 copy-start

commit v2 on v1

v2 whole, which is shorter than its diff:
```python
import jax
import jax.numpy as jnp
import numpy as np
from jax import lax
from jax.experimental import pallas as pl
from jax.experimental.pallas import tpu as pltpu
from jax.sharding import PartitionSpec as P

ORDER = 8
LANES = 128
WIDE = 256
PAD_ROWS = 176
PITCH = 40
CHUNK = 16
SHIFT = 40
BF = jnp.bfloat16
F32 = jnp.float32


def degree_signs():
    return np.concatenate(
        [np.full(((d + 1) * (d + 2) // 2,), (-1.0) ** d, np.float32) for d in range(ORDER + 1)]
    )


def lane_signs():
    signs = np.zeros((1, WIDE), np.float32)
    signs[0, : degree_signs().size] = degree_signs()
    return signs


def dot_nt(a, b):
    return lax.dot_general(a, b, (((1,), (1,)), ((), ())), preferred_element_type=F32)


def dot_nn(a, b):
    return lax.dot_general(a, b, (((1,), (0,)), ((), ())), preferred_element_type=F32)


def split(x):
    high = x.astype(BF)
    low = (x - high.astype(F32)).astype(BF)
    return high, low


def one_hot(ids, size):
    rows = lax.broadcasted_iota(jnp.int32, (size, ids.shape[1]), 0)
    return jnp.where(rows == ids, 1.0, 0.0).astype(BF)


def pair_hots(pairs_ref, batch, count, first, second):
    targets = pairs_ref[0, batch, 0:1, :]
    sources = pairs_ref[0, batch, 1:2, :]
    spots = lax.broadcasted_iota(jnp.int32, targets.shape, 1)
    targets = jnp.where(spots < count, targets, -1)
    return one_hot(targets, first), one_hot(sources, second)


def padded_rows(own):
    own = own.astype(F32)
    return jnp.concatenate([own, jnp.zeros((WIDE - own.shape[0], own.shape[1]), F32)], axis=0)


def scalar_row(read, count):
    lanes = lax.broadcasted_iota(jnp.int32, (1, LANES), 1)
    row = jnp.full((1, LANES), -1, jnp.int32)
    for i in range(count):
        row = jnp.where(lanes == i, read(i), row)
    return row


def pack_tiles(high, low, own):
    tail = high[:, LANES:] + pltpu.roll(low[:, LANES:], SHIFT, 1)
    tail = tail + pltpu.roll(own[:, LANES:], 2 * SHIFT, 1)
    return [high[:, :LANES], low[:, :LANES], own[:, :LANES], tail]


def unpack_tiles(tiles, coeffs):
    tail = tiles[3]
    lanes = lax.broadcasted_iota(jnp.int32, tail.shape, 1)
    parts = []
    for i in range(3):
        moved = tail if i == 0 else pltpu.roll(tail, LANES - i * SHIFT, 1)
        moved = jnp.where(lanes < coeffs - LANES, moved, 0.0)
        parts.append(jnp.concatenate([tiles[i], moved], axis=1).astype(BF))
    return parts


def prepare_kernel(
    batch_class, batch_count, me, group_send, own_ref, ops_hbm, group_ref, far_ref, far_send_ref,
    signs_ref, far_out, group_out, near_ops, rest_ops, ops_buf, low_table, high_table, near_mats,
    rest_mats, stage, in_sems, out_sems,
):
    batches = batch_class.shape[1]
    coeffs, cells = own_ref.shape
    near = near_mats.shape[0]
    group_batches = group_ref.shape[1]
    far_batches = far_ref.shape[1]
    group_slots = group_out.shape[0]
    far_slots = far_out.shape[0] // 4
    chunks = [(at, min(CHUNK, coeffs - at)) for at in range(0, coeffs, CHUNK)]
    copies = [
        pltpu.make_async_copy(
            ops_hbm.at[pl.ds(at, size)], ops_buf.at[pl.ds(at, size)], in_sems.at[i]
        )
        for i, (at, size) in enumerate(chunks)
    ]
    for copy in copies:
        copy.start()

    rows = lax.broadcasted_iota(jnp.int32, (2 * batches, WIDE), 0)
    lanes = lax.broadcasted_iota(jnp.int32, (2 * batches, WIDE), 1)
    wanted = jnp.zeros((2 * batches, WIDE), jnp.int32)
    for i in range(batches):
        wanted = jnp.where(rows == i, batch_class[0, i], wanted)
        wanted = jnp.where(rows == batches + i, batch_class[0, i] + LANES, wanted)
    hot = jnp.where(lanes == wanted, 1.0, 0.0).astype(BF)
    high_table[...] = jnp.zeros(high_table.shape, F32)
    low_table[coeffs * PITCH :, :] = jnp.zeros(((PAD_ROWS - coeffs) * PITCH, LANES), F32)

    signs = signs_ref[...]
    own = padded_rows(own_ref[...])
    own_half = own.astype(BF)
    sign_column = jnp.transpose(jnp.broadcast_to(signs, (LANES, WIDE)))
    flipped = (own * sign_column[:, :cells]).astype(BF)

    def gathered(pairs_ref, count_batches, first_batch, slots):
        counts = []
        for b in range(count_batches):
            hot_t, hot_u = pair_hots(
                pairs_ref, b, batch_count[0, first_batch + b], cells, slots
            )
            counts.append(dot_nt(hot_u, hot_t).astype(BF))
        return dot_nt(jnp.concatenate(counts, axis=0), flipped)

    far_sum = gathered(far_ref, far_batches, near + group_batches, far_slots)
    group_sum = gathered(group_ref, group_batches, near, group_slots)
    far_own = jnp.transpose(dot_nn(own_half, one_hot(far_send_ref[...], cells)))
    row = scalar_row(lambda i: group_send[0, me[0], i // 8, i % 8], group_slots)
    group_own = jnp.transpose(dot_nn(own_half, one_hot(row, cells)))[:group_slots]

    def keep(at, picked):
        low_table[pl.ds(at * PITCH, batches), :] = picked[:, :LANES]
        high_table[pl.ds(at * PITCH, batches), : coeffs - LANES] = picked[:, LANES:]

    for copy, (at, size) in zip(copies, chunks):
        copy.wait()
        for i in range(at, at + size, 2):
            if i + 1 < at + size:
                both = dot_nt(hot, jnp.concatenate([ops_buf[i], ops_buf[i + 1]], axis=1))
                keep(i, both[:batches])
                keep(i + 1, both[batches:])
            else:
                keep(i, dot_nt(hot[:batches, :LANES], ops_buf[i]))

    def matrix(i):
        low = low_table[pl.ds(i, PAD_ROWS, stride=PITCH), :]
        high = high_table[pl.ds(i, PAD_ROWS, stride=PITCH), :]
        return jnp.concatenate([low, high], axis=1).astype(BF)

    for i in range(batches - near):
        rest_mats[i] = matrix(near + i)
    rest_copy = pltpu.make_async_copy(rest_mats, rest_ops, out_sems.at[0])
    rest_copy.start()
    for i in range(near):
        near_mats[i] = matrix(i)
    near_copy = pltpu.make_async_copy(near_mats, near_ops, out_sems.at[1])
    near_copy.start()

    def back_terms(summed, count_batches, first_batch, slots):
        total = jnp.zeros((slots, PAD_ROWS), F32)
        for b in range(count_batches):
            high, low = split(summed[b * slots : (b + 1) * slots])
            both = dot_nt(jnp.concatenate([high, low], axis=0), rest_mats[first_batch + b])
            total = total + both[:slots] + both[slots:]
        total = total * signs[:, :PAD_ROWS]
        total = jnp.concatenate([total, jnp.zeros((slots, WIDE - PAD_ROWS), F32)], axis=1)
        high, low = split(total)
        return high.astype(F32), low.astype(F32)

    tiles = pack_tiles(*back_terms(far_sum, far_batches, group_batches, far_slots), far_own)
    for i in range(4):
        stage[pl.ds(i, far_slots, stride=4), :] = tiles[i]
    far_out[...] = stage[...].astype(BF)
    tiles = pack_tiles(*back_terms(group_sum, group_batches, 0, group_slots), group_own)
    group_out[...] = jnp.concatenate(tiles, axis=1).astype(BF)
    rest_copy.wait()
    near_copy.wait()


def near_kernel(
    batch_count, own_ref, near_ref, group_ref, far_ref, ops_ref, signs_ref, out_ref, counts_ref
):
    cells = own_ref.shape[1]
    near = ops_ref.shape[0]
    signs = signs_ref[...]
    own = padded_rows(own_ref[...])
    own_half = own.astype(BF)
    sign_column = jnp.transpose(jnp.broadcast_to(signs, (LANES, WIDE)))
    flipped = (own * sign_column[:, :cells]).astype(BF)
    forward, backward = [], []
    for b in range(near):
        hot_t, hot_u = pair_hots(near_ref, b, batch_count[0, b], cells, cells)
        forward.append(dot_nt(hot_t, hot_u).astype(BF))
        backward.append(dot_nt(hot_u, hot_t).astype(BF))
    ahead = dot_nt(jnp.concatenate(forward, axis=0), own_half)
    behind = dot_nt(jnp.concatenate(backward, axis=0), flipped)
    total = jnp.zeros((cells, PAD_ROWS), F32)
    mirrored = jnp.zeros((cells, PAD_ROWS), F32)
    for b in range(near):
        part = slice(b * cells, (b + 1) * cells)
        both = dot_nt(
            jnp.concatenate([*split(ahead[part]), *split(behind[part])], axis=0), ops_ref[b]
        )
        total = total + both[:cells] + both[cells : 2 * cells]
        mirrored = mirrored + both[2 * cells : 3 * cells] + both[3 * cells :]
    out_ref[...] = total + mirrored * signs[:, :PAD_ROWS]
    done = near
    for pairs_ref in (group_ref, far_ref):
        for b in range(pairs_ref.shape[1]):
            hot_t, hot_u = pair_hots(pairs_ref, b, batch_count[0, done], cells, LANES)
            counts_ref[done - near] = dot_nt(hot_t, hot_u).astype(BF)
            done += 1


def finish_kernel(
    me, group_send, near_sum, counts_ref, ops_ref, far_send_ref, far_in, group_in, out_ref, stage
):
    coeffs, cells = out_ref.shape
    far_slots = far_in.shape[0] // 4
    group_slots = group_in.shape[0]
    group_batches = counts_ref.shape[0] // 2
    stage[...] = far_in[...].astype(F32)
    tiles = [stage[pl.ds(i, far_slots, stride=4), :] for i in range(4)]
    far_high, far_low, far_arrived = unpack_tiles(tiles, coeffs)
    tiles = [group_in[:, i * LANES : (i + 1) * LANES].astype(F32) for i in range(4)]
    group_high, group_low, group_arrived = unpack_tiles(tiles, coeffs)

    total = near_sum[...]
    for first, arrived in ((0, group_arrived), (group_batches, far_arrived)):
        slots = arrived.shape[0]
        counts = [counts_ref[first + b][:, :slots] for b in range(group_batches)]
        summed = dot_nn(jnp.concatenate(counts, axis=0), arrived)
        for b in range(group_batches):
            high, low = split(summed[b * cells : (b + 1) * cells])
            both = dot_nt(jnp.concatenate([high, low], axis=0), ops_ref[first + b])
            total = total + both[:cells] + both[cells:]

    far_hot = one_hot(far_send_ref[...], cells)
    row = scalar_row(lambda i: group_send[0, me[0], i // 8, i % 8], group_slots)
    group_hot = one_hot(row, cells)[:, :group_slots]
    home = dot_nn(far_hot, far_high) + dot_nn(far_hot, far_low)
    home = home + dot_nn(group_hot, group_high) + dot_nn(group_hot, group_low)
    total = total + home[:, :PAD_ROWS]
    total = jnp.concatenate([total, jnp.zeros((cells, WIDE - PAD_ROWS), F32)], axis=1)
    out_ref[...] = jnp.transpose(total)[:coeffs]


def body(
    multipoles, operators, local_pairs, group_pairs, far_pairs, batch_class, batch_count,
    group_send, far_send,
):
    coeffs, cells = multipoles.shape
    batches = batch_class.shape[1]
    near = local_pairs.shape[1]
    rest = batches - near
    group_size = lax.axis_size("grp")
    ranges = lax.axis_size("cells")
    far_slots = far_send.shape[1] * far_send.shape[2]
    far_send = far_send.reshape(1, far_slots)
    group_slots = group_size * group_send.shape[3]
    me = lax.axis_index("grp").reshape(1)
    signs = jnp.asarray(lane_signs())
    smem = pl.BlockSpec(memory_space=pltpu.SMEM)
    vmem = pl.BlockSpec(memory_space=pltpu.VMEM)
    hbm = pl.BlockSpec(memory_space=pl.ANY)
    chunk_count = -(-coeffs // CHUNK)
    far_rows, group_rows, ops_near, ops_rest = pl.pallas_call(
        prepare_kernel,
        in_specs=[smem] * 4 + [vmem, hbm] + [vmem] * 4,
        out_specs=[vmem, vmem, hbm, hbm],
        out_shape=[
            jax.ShapeDtypeStruct((far_slots * 4, LANES), BF),
            jax.ShapeDtypeStruct((group_slots, 4 * LANES), BF),
            jax.ShapeDtypeStruct((near, PAD_ROWS, WIDE), BF),
            jax.ShapeDtypeStruct((rest, PAD_ROWS, WIDE), BF),
        ],
        scratch_shapes=[
            pltpu.VMEM(operators.shape, BF),
            pltpu.VMEM((PAD_ROWS * PITCH, LANES), F32),
            pltpu.VMEM((PAD_ROWS * PITCH, LANES), F32),
            pltpu.VMEM((near, PAD_ROWS, WIDE), BF),
            pltpu.VMEM((rest, PAD_ROWS, WIDE), BF),
            pltpu.VMEM((far_slots * 4, LANES), F32),
            pltpu.SemaphoreType.DMA((chunk_count,)),
            pltpu.SemaphoreType.DMA((2,)),
        ],
        compiler_params=pltpu.CompilerParams(vmem_limit_bytes=60 * 1024 * 1024),
        name="prepare",
    )(
        batch_class, batch_count, me, group_send, multipoles, operators, group_pairs, far_pairs,
        far_send, signs,
    )
    group_got = lax.all_to_all(
        group_rows.reshape(group_size, -1, 4 * LANES), "grp", split_axis=0, concat_axis=0, tiled=True
    ).reshape(group_rows.shape)
    far_got = lax.all_to_all(
        far_rows.reshape(ranges, -1, LANES), "cells", split_axis=0, concat_axis=0, tiled=True
    ).reshape(far_rows.shape)
    near_sum, counts = pl.pallas_call(
        near_kernel,
        in_specs=[smem] + [vmem] * 6,
        out_specs=[vmem, vmem],
        out_shape=[
            jax.ShapeDtypeStruct((cells, PAD_ROWS), F32),
            jax.ShapeDtypeStruct((rest, cells, LANES), BF),
        ],
        compiler_params=pltpu.CompilerParams(vmem_limit_bytes=24 * 1024 * 1024),
        cost_estimate=pl.CostEstimate(
            flops=20_000_000_000, bytes_accessed=40_000_000, transcendentals=0
        ),
        name="near",
    )(batch_count, multipoles, local_pairs, group_pairs, far_pairs, ops_near, signs)
    return pl.pallas_call(
        finish_kernel,
        in_specs=[smem] * 2 + [vmem] * 6,
        out_specs=vmem,
        out_shape=jax.ShapeDtypeStruct((coeffs, cells), F32),
        scratch_shapes=[pltpu.VMEM((far_slots * 4, LANES), F32)],
        compiler_params=pltpu.CompilerParams(vmem_limit_bytes=24 * 1024 * 1024),
        name="finish",
    )(me, group_send, near_sum, counts, ops_rest, far_send, far_got, group_got)


def solution(mesh):
    placed = (
        P(None, ("cells", "grp")),
        P(),
        P(("cells", "grp"), None, None, None),
        P(("cells", "grp"), None, None, None),
        P(("cells", "grp"), None, None, None),
        P(("cells", "grp"), None),
        P(("cells", "grp"), None),
        P("cells", None, None, None),
        P(("cells", "grp"), None, None),
    )
    return jax.shard_map(
        body, mesh=mesh, in_specs=placed, out_specs=P(None, ("cells", "grp")), check_vma=False
    )
```

time: 82.7 us -> 67.4 us (0.81)
  Pallas kernels: 30.2 us -> 17.7 us
  waiting for transfers between devices: 10 us -> 7.37 us
    pallas_call x3, Pallas kernels: 30.2 us -> 17.7 us  [the longest x1 10.4 us: body(): pl.pallas_call(prepare_kernel, in_specs=[smem] * 4 + [vmem, hbm] + [vmem]...]
    all_to_all x1, waiting for transfers between devices: 10 us -> 7.37 us  [body(): lax.all_to_all(far_rows.reshape(ranges, -1, LANES), 'cells', split_axis=0...]
where the time goes in v2:
time: 67.4 us; the launch traced here: 67 us
  starting transfers between devices  25 us (37%)
  Pallas kernels  17.7 us (26%)
  blocking collectives  15.3 us (23%)
  waiting for transfers between devices  7.37 us (11%)
  local copies, waits for them, and re-layouts  1.39 us (2%)
    all_to_all x1, starting transfers between devices, body(): lax.all_to_all(far_rows.reshape(ranges, -1, LANES), 'cells', split_axis=0...  25 us
    all_to_all x1, blocking collectives, body(): lax.all_to_all(group_rows.reshape(group_size, -1, 4 * LANES), 'grp', spli...  15.3 us
    pallas_call x1, Pallas kernels, body(): pl.pallas_call(prepare_kernel, in_specs=[smem] * 4 + [vmem, hbm] + [vmem]...  10.4 us
    all_to_all x1, waiting for transfers between devices, body(): lax.all_to_all(far_rows.reshape(ranges, -1, LANES), 'cells', split_axis=0...  7.37 us
    pallas_call x1, Pallas kernels, body(): pl.pallas_call(near_kernel, in_specs=[smem] + [vmem] * 6, out_specs=[vmem...  3.91 us
    pallas_call x1, Pallas kernels, body(): pl.pallas_call(finish_kernel, in_specs=[smem] * 2 + [vmem] * 6, out_specs...  3.45 us
    unnamed x20, local copies, waits for them, and re-layouts  1.39 us
  transfers between devices with their start and end apart: 1, of which 1 were waited for; matrix products, arithmetic and copies ran while one was open for 0% of the time, Pallas kernels for 6%

profile of v2, /device:TPU:1, one launch (start us, length us, event | category | flops | bytes accessed | tf_op | source)
XLA Modules:
  0.0 67.0 jit_solution(9578425406466625024)
XLA Ops:
  0.0 0.0 copy-start.2
  0.0 0.0 copy-start.3
  0.0 0.0 copy-start.4
  0.0 0.0 copy-start.6
  0.0 0.0 copy-start.7
  0.0 0.0 copy-start.9
  0.0 10.4 %prepare.1 = (bf16[512,128]{1,0:T(8,128)(2,1)}, bf16[64,512]{1,0:T(8,128)(2,1)}, bf16[16,176,256]{2,1,0:T(8,128)(2,1)}, bf16[16,176,256]{2,1,0:T(8,128)(2,1)}) custom-call(s32[1,32]{1,0:T(1,128)} %batch_class.1, s32[1,32]{1,0:T(1,128)} %batch_count.3, s32[1]{0:T(128)} %bitcast.me, s32[1,8,8,8]{3,2,1,0:T(8,128)} %group_send.3, bf16[165,128]{1,0:T(8,128)(2,1)} %own_ref.3, ...), custom_call_target="tpu_custom_call" | custom-call | tf_op jit(solution)/shard_map/prepare/pallas_call | solution.py:278
  10.4 15.3 %all_to_all.10 = bf16[8,8,512]{2,1,0:T(8,128)(2,1)S(1)} all-to-all(bf16[8,8,512]{2,1,0:T(8,128)(2,1)} %bitcast.11), channel_id=1, replica_groups=mesh['cells'=128,'grp'=8] {'grp'}, dimensions={0} | all-to-all | bytes 131072 | tf_op jit(solution)/shard_map/all_to_all | solution.py:304
  25.8 25.0 %all-to-all-start = ((bf16[128,4,128]{2,1,0:T(4,128)(2,1)}), bf16[128,4,128]{2,1,0:T(4,128)(2,1)S(1)}, u32[]{:S(2)}, u32[]{:S(2)}) async-start(bf16[128,4,128]{2,1,0:T(4,128)(2,1)} %bitcast.10), calls=%async_computation | async-start | bytes 262144 | tf_op jit(solution)/shard_map/all_to_all | solution.py:307
  50.8 0.0 copy-done.2
  50.8 0.0 copy-done.3
  50.8 0.0 copy-done.4
  50.9 0.0 copy-done.6
  50.9 0.0 copy-done.7
  50.9 0.0 copy-done.9
  50.9 0.0 copy-start.8
  50.9 1.4 %copy-done.8 = bf16[16,176,256]{2,1,0:T(8,128)(2,1)S(1)} copy-done((bf16[16,176,256]{2,1,0:T(8,128)(2,1)S(1)}, bf16[16,176,256]{2,1,0:T(8,128)(2,1)}, u32[]{:S(2)}) %copy-start.8) | copy-done | bytes 1441816
  52.2 0.0 copy-start
  52.2 0.0 copy-start.1
  52.3 0.0 copy-start.5
  52.3 3.9 %near.1 = (f32[128,176]{1,0:T(8,128)S(1)}, bf16[16,128,128]{2,1,0:T(8,128)(2,1)S(1)}) custom-call(s32[1,32]{1,0:T(1,128)S(1)} %copy-done.7, bf16[165,128]{1,0:T(8,128)(2,1)S(1)} %copy-done.2, s32[1,16,2,256]{3,2,1,0:T(2,128)S(1)} %copy-done.9, s32[1,8,2,256]{3,2,1,0:T(2,128)S(1)} %copy-done.3, s32[1,8,2,256]{3,2,1,0:T(2,128)S(1)} %copy-done.4, ...), custom_call_target="tpu_custom_call" | custom-call | flops 20000000000 | bytes 40000000 | tf_op jit(solution)/shard_map/near/pallas_call | solution.py:310
  56.2 7.4 %all-to-all-done = bf16[128,4,128]{2,1,0:T(4,128)(2,1)S(1)} async-done(((bf16[128,4,128]{2,1,0:T(4,128)(2,1)}), bf16[128,4,128]{2,1,0:T(4,128)(2,1)S(1)}, u32[]{:S(2)}, u32[]{:S(2)}) %all-to-all-start) | async-done | bytes 131104 | tf_op jit(solution)/shard_map/all_to_all | solution.py:307
  63.5 0.0 copy-done
  63.5 0.0 copy-done.1
  63.5 0.0 copy-done.5
  63.6 3.4 %finish.1 = f32[165,128]{1,0:T(8,128)} custom-call(s32[1]{0:T(128)} %bitcast.me, s32[1,8,8,8]{3,2,1,0:T(8,128)S(1)} %copy-done.1, f32[128,176]{1,0:T(8,128)S(1)} %get-tuple-element.12.near_sum, bf16[16,128,128]{2,1,0:T(8,128)(2,1)S(1)} %get-tuple-element.13.counts_ref, bf16[16,176,256]{2,1,0:T(8,128)(2,1)S(1)} %copy-done, s32[1,128]{1,0:T(1,128)S(1)} %bitcast.9, ...), custom_call_target="tpu_custom_call" | custom-call | tf_op jit(solution)/shard_map/finish/pallas_call | solution.py:324
Async XLA Ops:
  0.0 50.8 %copy-start.2 = (bf16[165,128]{1,0:T(8,128)(2,1)S(1)}, bf16[165,128]{1,0:T(8,128)(2,1)}, u32[]{:S(2)}) copy-start(bf16[165,128]{1,0:T(8,128)(2,1)} %own_ref.3) | copy-start | bytes 126724
  0.0 50.8 %copy-start.3 = (s32[1,8,2,256]{3,2,1,0:T(2,128)S(1)}, s32[1,8,2,256]{3,2,1,0:T(2,128)}, u32[]{:S(2)}) copy-start(s32[1,8,2,256]{3,2,1,0:T(2,128)} %group_ref.3) | copy-start | bytes 49156
  0.0 50.8 %copy-start.4 = (s32[1,8,2,256]{3,2,1,0:T(2,128)S(1)}, s32[1,8,2,256]{3,2,1,0:T(2,128)}, u32[]{:S(2)}) copy-start(s32[1,8,2,256]{3,2,1,0:T(2,128)} %far_ref.3) | copy-start | bytes 49156
  0.0 50.8 %copy-start.6 = (f32[1,256]{1,0:T(1,128)S(1)}, f32[1,256]{1,0:T(1,128)}, u32[]{:S(2)}) copy-start(f32[1,256]{1,0:T(1,128)} %constant.6.clone.signs_ref) | copy-start | bytes 3076
  0.0 50.8 %copy-start.7 = (s32[1,32]{1,0:T(1,128)S(1)}, s32[1,32]{1,0:T(1,128)}, u32[]{:S(2)}) copy-start(s32[1,32]{1,0:T(1,128)} %batch_count.3) | copy-start | bytes 388
  0.0 50.8 %copy-start.9 = (s32[1,16,2,256]{3,2,1,0:T(2,128)S(1)}, s32[1,16,2,256]{3,2,1,0:T(2,128)}, u32[]{:S(2)}) copy-start(s32[1,16,2,256]{3,2,1,0:T(2,128)} %near_ref.1) | copy-start | bytes 98308
  25.8 37.8 %all-to-all-start = ((bf16[128,4,128]{2,1,0:T(4,128)(2,1)}), bf16[128,4,128]{2,1,0:T(4,128)(2,1)S(1)}, u32[]{:S(2)}, u32[]{:S(2)}) async-start(bf16[128,4,128]{2,1,0:T(4,128)(2,1)} %bitcast.10), calls=%async_computation | async-start | bytes 262144 | tf_op jit(solution)/shard_map/all_to_all | solution.py:307
  50.9 1.4 %copy-start.8 = (bf16[16,176,256]{2,1,0:T(8,128)(2,1)S(1)}, bf16[16,176,256]{2,1,0:T(8,128)(2,1)}, u32[]{:S(2)}) copy-start(bf16[16,176,256]{2,1,0:T(8,128)(2,1)} %get-tuple-element.11.ops_ref) | copy-start | bytes 4325380
  52.2 11.3 %copy-start = (bf16[16,176,256]{2,1,0:T(8,128)(2,1)S(1)}, bf16[16,176,256]{2,1,0:T(8,128)(2,1)}, u32[]{:S(2)}) copy-start(bf16[16,176,256]{2,1,0:T(8,128)(2,1)} %get-tuple-element.14.ops_ref) | copy-start | bytes 4325380
  52.2 11.3 %copy-start.1 = (s32[1,8,8,8]{3,2,1,0:T(8,128)S(1)}, s32[1,8,8,8]{3,2,1,0:T(8,128)}, u32[]{:S(2)}) copy-start(s32[1,8,8,8]{3,2,1,0:T(8,128)} %group_send.3) | copy-start | bytes 6148
  52.3 11.3 %copy-start.5 = (s32[1,128,1]{1,2,0:T(1,128)S(1)}, s32[1,128,1]{1,2,0:T(1,128)}, u32[]{:S(2)}) copy-start(s32[1,128,1]{1,2,0:T(1,128)} %param.18) | copy-start | bytes 1540

commit v3 on v2

v3 whole, which is shorter than its diff:
```python
import jax
import jax.numpy as jnp
from jax import lax
from jax.experimental import pallas as pl
from jax.experimental.pallas import tpu as pltpu
from jax.sharding import PartitionSpec as P

ORDER = 8
LANES = 128
WIDE = 256
PAD_ROWS = 176
PITCH = 40
CHUNK = 64
SHIFT = 40
MIB = 1024 * 1024
NEAR_LIMIT = 24 * MIB
BF = jnp.bfloat16
F32 = jnp.float32


def signs_of(index):
    degree = jnp.zeros(index.shape, jnp.int32)
    count = 0
    for d in range(ORDER + 1):
        count += (d + 1) * (d + 2) // 2
        degree = degree + jnp.where(index >= count, 1, 0)
    sign = jnp.where(degree % 2 == 0, 1.0, -1.0)
    return jnp.where(index < count, sign, 0.0)


def lane_signs():
    return signs_of(lax.broadcasted_iota(jnp.int32, (1, WIDE), 1))


def own_tables(own):
    own = own.astype(F32)
    own = jnp.concatenate([own, jnp.zeros((WIDE - own.shape[0], own.shape[1]), F32)], axis=0)
    signs = signs_of(lax.broadcasted_iota(jnp.int32, own.shape, 0))
    return own.astype(BF), (own * signs).astype(BF)


def dot_nt(a, b):
    return lax.dot_general(a, b, (((1,), (1,)), ((), ())), preferred_element_type=F32)


def dot_nn(a, b):
    return lax.dot_general(a, b, (((1,), (0,)), ((), ())), preferred_element_type=F32)


def split(x):
    high = x.astype(BF)
    low = (x - high.astype(F32)).astype(BF)
    return high, low


def one_hot(ids, size):
    rows = lax.broadcasted_iota(jnp.int32, (size, ids.shape[1]), 0)
    return jnp.where(rows == ids, 1.0, 0.0).astype(BF)


def pair_hots(pairs_ref, batch, count, first, second):
    targets = pairs_ref[0, batch, 0:1, :]
    sources = pairs_ref[0, batch, 1:2, :]
    spots = lax.broadcasted_iota(jnp.int32, targets.shape, 1)
    targets = jnp.where(spots < count, targets, -1)
    return one_hot(targets, first), one_hot(sources, second)


def scalar_row(read, count):
    lanes = lax.broadcasted_iota(jnp.int32, (1, LANES), 1)
    row = jnp.full((1, LANES), -1, jnp.int32)
    for i in range(count):
        row = jnp.where(lanes == i, read(i), row)
    return row


def pack_tiles(high, low, own):
    tail = high[:, LANES:] + pltpu.roll(low[:, LANES:], SHIFT, 1)
    tail = tail + pltpu.roll(own[:, LANES:], 2 * SHIFT, 1)
    return [high[:, :LANES], low[:, :LANES], own[:, :LANES], tail]


def unpack_tiles(tiles, coeffs):
    tail = tiles[3]
    lanes = lax.broadcasted_iota(jnp.int32, tail.shape, 1)
    parts = []
    for i in range(3):
        moved = tail if i == 0 else pltpu.roll(tail, LANES - i * SHIFT, 1)
        moved = jnp.where(lanes < coeffs - LANES, moved, 0.0)
        parts.append(jnp.concatenate([tiles[i], moved], axis=1).astype(BF))
    return parts


def prepare_kernel(
    me, class_hbm, count_hbm, send_hbm, own_hbm, ops_hbm, group_hbm, far_hbm, far_send_hbm,
    far_out, group_out, near_ops, far_ops, batch_class, batch_count, group_send, own_ref, group_ref,
    far_ref, far_send_ref, ops_buf, low_table, high_table, near_mats, far_mats, stage, small_sems,
    in_sems, out_sems,
):
    batches = batch_class.shape[1]
    coeffs, cells = own_ref.shape
    first_far = near_mats.shape[0]
    group_batches = group_ref.shape[1]
    far_batches = far_ref.shape[1]
    first_group = first_far - group_batches
    group_slots = group_out.shape[0]
    far_slots = far_out.shape[0] // 4
    small = [
        pltpu.make_async_copy(source, target, small_sems.at[i])
        for i, (source, target) in enumerate(
            (
                (class_hbm, batch_class),
                (count_hbm, batch_count),
                (send_hbm, group_send),
                (own_hbm, own_ref),
                (group_hbm, group_ref),
                (far_hbm, far_ref),
                (far_send_hbm, far_send_ref),
            )
        )
    ]
    for copy in small:
        copy.start()
    chunks = [(at, min(CHUNK, coeffs - at)) for at in range(0, coeffs, CHUNK)]
    copies = [
        pltpu.make_async_copy(
            ops_hbm.at[pl.ds(at, size)], ops_buf.at[pl.ds(at, size)], in_sems.at[i]
        )
        for i, (at, size) in enumerate(chunks)
    ]
    for copy in copies:
        copy.start()

    high_table[...] = jnp.zeros(high_table.shape, F32)
    low_table[coeffs * PITCH :, :] = jnp.zeros(((PAD_ROWS - coeffs) * PITCH, LANES), F32)
    for copy in small:
        copy.wait()

    rows = lax.broadcasted_iota(jnp.int32, (2 * batches, WIDE), 0)
    lanes = lax.broadcasted_iota(jnp.int32, (2 * batches, WIDE), 1)
    wanted = jnp.zeros((2 * batches, WIDE), jnp.int32)
    for i in range(batches):
        wanted = jnp.where(rows == i, batch_class[0, i], wanted)
        wanted = jnp.where(rows == batches + i, batch_class[0, i] + LANES, wanted)
    hot = jnp.where(lanes == wanted, 1.0, 0.0).astype(BF)

    own_half, flipped = own_tables(own_ref[...])

    def gathered(pairs_ref, count_batches, first_batch, slots):
        counts = []
        for b in range(count_batches):
            hot_t, hot_u = pair_hots(
                pairs_ref, b, batch_count[0, first_batch + b], cells, slots
            )
            counts.append(dot_nt(hot_u, hot_t).astype(BF))
        return dot_nt(jnp.concatenate(counts, axis=0), flipped)

    far_sum = gathered(far_ref, far_batches, first_far, far_slots)
    group_sum = gathered(group_ref, group_batches, first_group, group_slots)
    far_own = jnp.transpose(dot_nn(own_half, one_hot(far_send_ref[...], cells)))
    row = scalar_row(lambda i: group_send[0, me[0], i // 8, i % 8], group_slots)
    group_own = jnp.transpose(dot_nn(own_half, one_hot(row, cells)))[:group_slots]

    def keep(at, picked):
        low_table[pl.ds(at * PITCH, batches), :] = picked[:, :LANES]
        high_table[pl.ds(at * PITCH, batches), : coeffs - LANES] = picked[:, LANES:]

    outs = []

    def take_out(c):
        at = chunks[c][0]
        size = min(CHUNK, PAD_ROWS - at)
        for i in range(batches):
            low = low_table[pl.ds(at * PITCH + i, size, stride=PITCH), :]
            high = high_table[pl.ds(at * PITCH + i, size, stride=PITCH), :]
            mats, place = (near_mats, i) if i < first_far else (far_mats, i - first_far)
            mats[place, at : at + size, :] = jnp.concatenate([low, high], axis=1).astype(BF)
        for k, (mats, target) in enumerate(((near_mats, near_ops), (far_mats, far_ops))):
            out = pltpu.make_async_copy(
                mats.at[:, pl.ds(at, size), :],
                target.at[:, pl.ds(at, size), :],
                out_sems.at[2 * c + k],
            )
            out.start()
            outs.append(out)

    for c, (copy, (at, size)) in enumerate(zip(copies, chunks)):
        copy.wait()
        for i in range(at, at + size, 2):
            if i + 1 < at + size:
                both = dot_nt(hot, jnp.concatenate([ops_buf[i], ops_buf[i + 1]], axis=1))
                keep(i, both[:batches])
                keep(i + 1, both[batches:])
            else:
                keep(i, dot_nt(hot[:batches, :LANES], ops_buf[i]))
        if c > 0:
            take_out(c - 1)
    take_out(len(chunks) - 1)

    signs = lane_signs()

    def back_terms(summed, mats, count_batches, first, slots):
        total = jnp.zeros((slots, PAD_ROWS), F32)
        for b in range(count_batches):
            high, low = split(summed[b * slots : (b + 1) * slots])
            both = dot_nt(jnp.concatenate([high, low], axis=0), mats[first + b])
            total = total + both[:slots] + both[slots:]
        total = total * signs[:, :PAD_ROWS]
        total = jnp.concatenate([total, jnp.zeros((slots, WIDE - PAD_ROWS), F32)], axis=1)
        high, low = split(total)
        return high.astype(F32), low.astype(F32)

    tiles = pack_tiles(*back_terms(far_sum, far_mats, far_batches, 0, far_slots), far_own)
    for i in range(4):
        stage[pl.ds(i, far_slots, stride=4), :] = tiles[i]
    far_out[...] = stage[...].astype(BF)
    tiles = pack_tiles(
        *back_terms(group_sum, near_mats, group_batches, first_group, group_slots), group_own
    )
    group_out[...] = jnp.concatenate(tiles, axis=1).astype(BF)
    for out in outs:
        out.wait()


def forward_terms(total, counts, arrived, matrix):
    cells = total.shape[0]
    summed = dot_nn(jnp.concatenate(counts, axis=0), arrived)
    for b in range(len(counts)):
        high, low = split(summed[b * cells : (b + 1) * cells])
        both = dot_nt(jnp.concatenate([high, low], axis=0), matrix(b))
        total = total + both[:cells] + both[cells:]
    return total


def near_kernel(
    me, batch_count, group_send, own_ref, near_ref, group_ref, far_ref, group_in, ops_hbm,
    out_ref, counts_ref, ops_ref, sems,
):
    coeffs, cells = own_ref.shape
    near = near_ref.shape[1]
    group_slots = group_in.shape[0]
    parts = sems.shape[0]
    size = ops_hbm.shape[0] // parts
    copies = [
        pltpu.make_async_copy(
            ops_hbm.at[pl.ds(i * size, size)], ops_ref.at[pl.ds(i * size, size)], sems.at[i]
        )
        for i in range(parts)
    ]
    for copy in copies:
        copy.start()
    own_half, flipped = own_tables(own_ref[...])
    forward, backward, remote = [], [], []
    for b in range(near):
        hot_t, hot_u = pair_hots(near_ref, b, batch_count[0, b], cells, cells)
        forward.append(dot_nt(hot_t, hot_u).astype(BF))
        backward.append(dot_nt(hot_u, hot_t).astype(BF))
    ahead = dot_nt(jnp.concatenate(forward, axis=0), own_half)
    behind = dot_nt(jnp.concatenate(backward, axis=0), flipped)
    done = near
    for b in range(group_ref.shape[1]):
        hot_t, hot_u = pair_hots(group_ref, b, batch_count[0, done], cells, group_slots)
        remote.append(dot_nt(hot_t, hot_u).astype(BF))
        done += 1
    for b in range(far_ref.shape[1]):
        hot_t, hot_u = pair_hots(far_ref, b, batch_count[0, done], cells, LANES)
        counts_ref[b] = dot_nt(hot_t, hot_u).astype(BF)
        done += 1
    total = jnp.zeros((cells, PAD_ROWS), F32)
    mirrored = jnp.zeros((cells, PAD_ROWS), F32)
    for b in range(near):
        if b % size == 0:
            copies[b // size].wait()
        part = slice(b * cells, (b + 1) * cells)
        both = dot_nt(
            jnp.concatenate([*split(ahead[part]), *split(behind[part])], axis=0), ops_ref[b]
        )
        total = total + both[:cells] + both[cells : 2 * cells]
        mirrored = mirrored + both[2 * cells : 3 * cells] + both[3 * cells :]
    total = total + mirrored * lane_signs()[:, :PAD_ROWS]
    for copy in copies[-(-near // size) :]:
        copy.wait()
    tiles = [group_in[:, i * LANES : (i + 1) * LANES].astype(F32) for i in range(4)]
    high, low, arrived = unpack_tiles(tiles, coeffs)
    total = forward_terms(total, remote, arrived, lambda b: ops_ref[near + b])
    row = scalar_row(lambda i: group_send[0, me[0], i // 8, i % 8], group_slots)
    hot = one_hot(row, cells)[:, :group_slots]
    out_ref[...] = total + (dot_nn(hot, high) + dot_nn(hot, low))[:, :PAD_ROWS]


def finish_kernel(near_sum, counts_ref, ops_ref, far_send_ref, far_in, out_ref, stage):
    coeffs, cells = out_ref.shape
    far_slots = far_in.shape[0] // 4
    stage[...] = far_in[...].astype(F32)
    tiles = [stage[pl.ds(i, far_slots, stride=4), :] for i in range(4)]
    high, low, arrived = unpack_tiles(tiles, coeffs)
    counts = [counts_ref[b] for b in range(counts_ref.shape[0])]
    total = forward_terms(near_sum[...], counts, arrived, lambda b: ops_ref[b])
    hot = one_hot(far_send_ref[...], cells)
    total = total + (dot_nn(hot, high) + dot_nn(hot, low))[:, :PAD_ROWS]
    total = jnp.concatenate([total, jnp.zeros((cells, WIDE - PAD_ROWS), F32)], axis=1)
    out_ref[...] = jnp.transpose(total)[:coeffs]


def body(
    multipoles, operators, local_pairs, group_pairs, far_pairs, batch_class, batch_count,
    group_send, far_send,
):
    coeffs, cells = multipoles.shape
    batches = batch_class.shape[1]
    far_batches = far_pairs.shape[1]
    first_far = batches - far_batches
    group_size = lax.axis_size("grp")
    ranges = lax.axis_size("cells")
    far_slots = far_send.shape[1] * far_send.shape[2]
    far_send = far_send.reshape(1, far_slots)
    group_slots = group_size * group_send.shape[3]
    me = lax.axis_index("grp").reshape(1)
    smem = pl.BlockSpec(memory_space=pltpu.SMEM)
    vmem = pl.BlockSpec(memory_space=pltpu.VMEM)
    hbm = pl.BlockSpec(memory_space=pl.ANY)
    chunk_count = -(-coeffs // CHUNK)
    far_rows, group_rows, ops_near, ops_far = pl.pallas_call(
        prepare_kernel,
        in_specs=[smem] + [hbm] * 8,
        out_specs=[vmem, vmem, hbm, hbm],
        out_shape=[
            jax.ShapeDtypeStruct((far_slots * 4, LANES), BF),
            jax.ShapeDtypeStruct((group_slots, 4 * LANES), BF),
            jax.ShapeDtypeStruct((first_far, PAD_ROWS, WIDE), BF),
            jax.ShapeDtypeStruct((far_batches, PAD_ROWS, WIDE), BF),
        ],
        scratch_shapes=[
            pltpu.SMEM(batch_class.shape, jnp.int32),
            pltpu.SMEM(batch_count.shape, jnp.int32),
            pltpu.SMEM(group_send.shape, jnp.int32),
            pltpu.VMEM(multipoles.shape, BF),
            pltpu.VMEM(group_pairs.shape, jnp.int32),
            pltpu.VMEM(far_pairs.shape, jnp.int32),
            pltpu.VMEM(far_send.shape, jnp.int32),
            pltpu.VMEM(operators.shape, BF),
            pltpu.VMEM((PAD_ROWS * PITCH, LANES), F32),
            pltpu.VMEM((PAD_ROWS * PITCH, LANES), F32),
            pltpu.VMEM((first_far, PAD_ROWS, WIDE), BF),
            pltpu.VMEM((far_batches, PAD_ROWS, WIDE), BF),
            pltpu.VMEM((far_slots * 4, LANES), F32),
            pltpu.SemaphoreType.DMA((7,)),
            pltpu.SemaphoreType.DMA((chunk_count,)),
            pltpu.SemaphoreType.DMA((2 * chunk_count,)),
        ],
        compiler_params=pltpu.CompilerParams(vmem_limit_bytes=60 * MIB),
        name="prepare",
    )(
        me, batch_class, batch_count, group_send, multipoles, operators, group_pairs, far_pairs,
        far_send,
    )
    group_got = lax.all_to_all(
        group_rows.reshape(group_size, -1, 4 * LANES), "grp", split_axis=0, concat_axis=0, tiled=True
    ).reshape(group_rows.shape)
    far_got = lax.all_to_all(
        far_rows.reshape(ranges, -1, LANES), "cells", split_axis=0, concat_axis=0, tiled=True
    ).reshape(far_rows.shape)
    near_sum, counts = pl.pallas_call(
        near_kernel,
        in_specs=[smem] * 3 + [vmem] * 5 + [hbm],
        out_specs=[vmem, vmem],
        out_shape=[
            jax.ShapeDtypeStruct((cells, PAD_ROWS), F32),
            jax.ShapeDtypeStruct((far_batches, cells, LANES), BF),
        ],
        scratch_shapes=[
            pltpu.VMEM((first_far, PAD_ROWS, WIDE), BF),
            pltpu.SemaphoreType.DMA((3,)),
        ],
        compiler_params=pltpu.CompilerParams(vmem_limit_bytes=NEAR_LIMIT),
        cost_estimate=pl.CostEstimate(
            flops=20_000_000_000, bytes_accessed=40_000_000, transcendentals=0
        ),
        name="near",
    )(
        me, batch_count, group_send, multipoles, local_pairs, group_pairs, far_pairs, group_got,
        ops_near,
    )
    return pl.pallas_call(
        finish_kernel,
        in_specs=[vmem] * 5,
        out_specs=vmem,
        out_shape=jax.ShapeDtypeStruct((coeffs, cells), F32),
        scratch_shapes=[pltpu.VMEM((far_slots * 4, LANES), F32)],
        compiler_params=pltpu.CompilerParams(vmem_limit_bytes=24 * MIB),
        name="finish",
    )(near_sum, counts, ops_far, far_send, far_got)


def solution(mesh):
    placed = (
        P(None, ("cells", "grp")),
        P(),
        P(("cells", "grp"), None, None, None),
        P(("cells", "grp"), None, None, None),
        P(("cells", "grp"), None, None, None),
        P(("cells", "grp"), None),
        P(("cells", "grp"), None),
        P("cells", None, None, None),
        P(("cells", "grp"), None, None),
    )
    return jax.shard_map(
        body, mesh=mesh, in_specs=placed, out_specs=P(None, ("cells", "grp")), check_vma=False
    )
```

time: 67.4 us -> 63.6 us (0.944)
  waiting for transfers between devices: 7.37 us -> 3.86 us
    all_to_all x1, waiting for transfers between devices: 7.37 us -> 3.86 us  [body(): lax.all_to_all(far_rows.reshape(ranges, -1, LANES), 'cells', split_axis=0...]
    unnamed x20 -> x18, local copies, waits for them, and re-layouts: 1.39 us -> 1.63 us
  transfers between devices with their start and end apart: 1 -> 1, of which waited for: 1 -> 1; matrix products, arithmetic and copies ran while one was open for 0% -> 0% of each run, Pallas kernels for 6% -> 11%
where the time goes in v3:
time: 63.6 us; the launch traced here: 63.3 us
  starting transfers between devices  25 us (39%)
  Pallas kernels  17.3 us (27%)
  blocking collectives  15.3 us (24%)
  waiting for transfers between devices  3.86 us (6%)
  local copies, waits for them, and re-layouts  1.63 us (3%)
    all_to_all x1, starting transfers between devices, body(): lax.all_to_all(far_rows.reshape(ranges, -1, LANES), 'cells', split_axis=0...  25 us
    all_to_all x1, blocking collectives, body(): lax.all_to_all(group_rows.reshape(group_size, -1, 4 * LANES), 'grp', spli...  15.3 us
    pallas_call x1, Pallas kernels, body(): pl.pallas_call(prepare_kernel, in_specs=[smem] + [hbm] * 8, out_specs=[vm...  8.58 us
    pallas_call x1, Pallas kernels, body(): pl.pallas_call(near_kernel, in_specs=[smem] * 3 + [vmem] * 5 + [hbm], out...  7.18 us
    all_to_all x1, waiting for transfers between devices, body(): lax.all_to_all(far_rows.reshape(ranges, -1, LANES), 'cells', split_axis=0...  3.86 us
    unnamed x18, local copies, waits for them, and re-layouts  1.63 us
    pallas_call x1, Pallas kernels, body(): pl.pallas_call(finish_kernel, in_specs=[vmem] * 5, out_specs=vmem, out_sh...  1.53 us
  transfers between devices with their start and end apart: 1, of which 1 were waited for; matrix products, arithmetic and copies ran while one was open for 0% of the time, Pallas kernels for 11%

profile of v3, /device:TPU:1, one launch (start us, length us, event | category | flops | bytes accessed | tf_op | source)
XLA Modules:
  0.0 63.3 jit_solution(18017336604388878693)
XLA Ops:
  0.0 0.0 copy-start.2
  0.0 0.0 copy-start.6
  0.0 0.0 copy-start.4
  0.0 0.0 copy-start.3
  0.0 0.0 copy-start.1
  0.0 0.0 copy-start.8
  0.0 8.6 %prepare.1 = (bf16[512,128]{1,0:T(8,128)(2,1)}, bf16[64,512]{1,0:T(8,128)(2,1)}, bf16[24,176,256]{2,1,0:T(8,128)(2,1)}, bf16[8,176,256]{2,1,0:T(8,128)(2,1)}) custom-call(s32[1]{0:T(128)} %bitcast.me, s32[1,32]{1,0:T(1,128)} %class_hbm.1, s32[1,32]{1,0:T(1,128)} %batch_count.1, s32[1,8,8,8]{3,2,1,0:T(8,128)} %group_send.1, bf16[165,128]{1,0:T(8,128)(2,1)} %own_ref.1, ...), custom_call_target="tpu_custom_call" | custom-call | tf_op jit(solution)/shard_map/prepare/pallas_call | solution.py:323
  8.6 15.3 %all_to_all.10 = bf16[8,8,512]{2,1,0:T(8,128)(2,1)S(1)} all-to-all(bf16[8,8,512]{2,1,0:T(8,128)(2,1)} %bitcast.11), channel_id=1, replica_groups=mesh['cells'=128,'grp'=8] {'grp'}, dimensions={0} | all-to-all | bytes 131072 | tf_op jit(solution)/shard_map/all_to_all | solution.py:357
  24.0 25.0 %all-to-all-start.1 = ((bf16[128,4,128]{2,1,0:T(4,128)(2,1)}), bf16[128,4,128]{2,1,0:T(4,128)(2,1)S(1)}, u32[]{:S(2)}, u32[]{:S(2)}) async-start(bf16[128,4,128]{2,1,0:T(4,128)(2,1)} %bitcast.10), calls=%async_computation.1 | async-start | bytes 262144 | tf_op jit(solution)/shard_map/all_to_all | solution.py:360
  49.0 0.0 copy-done.2
  49.0 0.0 copy-done.6
  49.0 0.0 copy-done.4
  49.0 0.0 copy-done.3
  49.1 0.0 copy-done.1
  49.1 0.0 copy-done.8
  49.1 0.0 copy-start.7
  49.1 1.6 %copy-done.7 = bf16[24,176,256]{2,1,0:T(8,128)(2,1)S(1)} copy-done((bf16[24,176,256]{2,1,0:T(8,128)(2,1)S(1)}, bf16[24,176,256]{2,1,0:T(8,128)(2,1)}, u32[]{:S(2)}) %copy-start.7) | copy-done | bytes 2162712
  50.7 0.0 copy-start
  50.7 0.0 copy-start.5
  50.7 7.2 %near.1 = (f32[128,176]{1,0:T(8,128)S(1)}, bf16[8,128,128]{2,1,0:T(8,128)(2,1)S(1)}) custom-call(s32[1]{0:T(128)} %bitcast.me, s32[1,32]{1,0:T(1,128)S(1)} %copy-done.6, s32[1,8,8,8]{3,2,1,0:T(8,128)S(1)} %copy-done.2, bf16[165,128]{1,0:T(8,128)(2,1)S(1)} %copy-done.1, s32[1,16,2,256]{3,2,1,0:T(2,128)S(1)} %copy-done.8, s32[1,8,2,256]{3,2,1,0:T(2,128)S(1)} %copy-done.3, ...), custom_call_target="tpu_custom_call" | custom-call | flops 20000000000 | bytes 40000000 | tf_op jit(solution)/shard_map/near/pallas_call | solution.py:363
  57.9 3.9 %all-to-all-done.1 = bf16[128,4,128]{2,1,0:T(4,128)(2,1)S(1)} async-done(((bf16[128,4,128]{2,1,0:T(4,128)(2,1)}), bf16[128,4,128]{2,1,0:T(4,128)(2,1)S(1)}, u32[]{:S(2)}, u32[]{:S(2)}) %all-to-all-start.1) | async-done | bytes 131104 | tf_op jit(solution)/shard_map/all_to_all | solution.py:360
  61.7 0.0 copy-done
  61.8 0.0 copy-done.5
  61.8 1.5 %finish.1 = f32[165,128]{1,0:T(8,128)} custom-call(f32[128,176]{1,0:T(8,128)S(1)} %get-tuple-element.13.near_sum, bf16[8,128,128]{2,1,0:T(8,128)(2,1)S(1)} %get-tuple-element.14.counts_ref, bf16[8,176,256]{2,1,0:T(8,128)(2,1)S(1)} %copy-done, s32[1,128]{1,0:T(1,128)S(1)} %bitcast.9, bf16[512,128]{1,0:T(8,128)(2,1)S(1)} %bitcast.6), custom_call_target="tpu_custom_call" | custom-call | tf_op jit(solution)/shard_map/finish/pallas_call | solution.py:384
Async XLA Ops:
  0.0 49.0 %copy-start.2 = (s32[1,8,8,8]{3,2,1,0:T(8,128)S(1)}, s32[1,8,8,8]{3,2,1,0:T(8,128)}, u32[]{:S(2)}) copy-start(s32[1,8,8,8]{3,2,1,0:T(8,128)} %group_send.1) | copy-start | bytes 6148
  0.0 49.0 %copy-start.6 = (s32[1,32]{1,0:T(1,128)S(1)}, s32[1,32]{1,0:T(1,128)}, u32[]{:S(2)}) copy-start(s32[1,32]{1,0:T(1,128)} %batch_count.1) | copy-start | bytes 388
  0.0 49.0 %copy-start.4 = (s32[1,8,2,256]{3,2,1,0:T(2,128)S(1)}, s32[1,8,2,256]{3,2,1,0:T(2,128)}, u32[]{:S(2)}) copy-start(s32[1,8,2,256]{3,2,1,0:T(2,128)} %far_ref.1) | copy-start | bytes 49156
  0.0 49.0 %copy-start.3 = (s32[1,8,2,256]{3,2,1,0:T(2,128)S(1)}, s32[1,8,2,256]{3,2,1,0:T(2,128)}, u32[]{:S(2)}) copy-start(s32[1,8,2,256]{3,2,1,0:T(2,128)} %group_ref.1) | copy-start | bytes 49156
  0.0 49.0 %copy-start.1 = (bf16[165,128]{1,0:T(8,128)(2,1)S(1)}, bf16[165,128]{1,0:T(8,128)(2,1)}, u32[]{:S(2)}) copy-start(bf16[165,128]{1,0:T(8,128)(2,1)} %own_ref.1) | copy-start | bytes 126724
  0.0 49.0 %copy-start.8 = (s32[1,16,2,256]{3,2,1,0:T(2,128)S(1)}, s32[1,16,2,256]{3,2,1,0:T(2,128)}, u32[]{:S(2)}) copy-start(s32[1,16,2,256]{3,2,1,0:T(2,128)} %near_ref.1) | copy-start | bytes 98308
  24.0 37.8 %all-to-all-start.1 = ((bf16[128,4,128]{2,1,0:T(4,128)(2,1)}), bf16[128,4,128]{2,1,0:T(4,128)(2,1)S(1)}, u32[]{:S(2)}, u32[]{:S(2)}) async-start(bf16[128,4,128]{2,1,0:T(4,128)(2,1)} %bitcast.10), calls=%async_computation.1 | async-start | bytes 262144 | tf_op jit(solution)/shard_map/all_to_all | solution.py:360
  49.1 1.6 %copy-start.7 = (bf16[24,176,256]{2,1,0:T(8,128)(2,1)S(1)}, bf16[24,176,256]{2,1,0:T(8,128)(2,1)}, u32[]{:S(2)}) copy-start(bf16[24,176,256]{2,1,0:T(8,128)(2,1)} %get-tuple-element.12.ops_hbm) | copy-start | bytes 6488068
  50.7 11.1 %copy-start = (bf16[8,176,256]{2,1,0:T(8,128)(2,1)S(1)}, bf16[8,176,256]{2,1,0:T(8,128)(2,1)}, u32[]{:S(2)}) copy-start(bf16[8,176,256]{2,1,0:T(8,128)(2,1)} %get-tuple-element.15.ops_ref) | copy-start | bytes 2162692
  50.7 11.1 %copy-start.5 = (s32[1,128,1]{1,2,0:T(1,128)S(1)}, s32[1,128,1]{1,2,0:T(1,128)}, u32[]{:S(2)}) copy-start(s32[1,128,1]{1,2,0:T(1,128)} %param.17) | copy-start | bytes 1540

commit v4 on v3

--- a/solution.py
+++ b/solution.py
@@ -10,10 +10,9 @@
 WIDE = 256
 PAD_ROWS = 176
 PITCH = 40
-CHUNK = 64
+CHUNKS = (0, 96)
 SHIFT = 40
 MIB = 1024 * 1024
-NEAR_LIMIT = 24 * MIB
 BF = jnp.bfloat16
 F32 = jnp.float32
 
@@ -93,16 +92,15 @@
 
 def prepare_kernel(
     me, class_hbm, count_hbm, send_hbm, own_hbm, ops_hbm, group_hbm, far_hbm, far_send_hbm,
-    far_out, group_out, near_ops, far_ops, batch_class, batch_count, group_send, own_ref, group_ref,
-    far_ref, far_send_ref, ops_buf, low_table, high_table, near_mats, far_mats, stage, small_sems,
+    far_out, group_out, near_ops, rest_ops, batch_class, batch_count, group_send, own_ref, group_ref,
+    far_ref, far_send_ref, ops_buf, low_table, high_table, near_mats, rest_mats, stage, small_sems,
     in_sems, out_sems,
 ):
     batches = batch_class.shape[1]
     coeffs, cells = own_ref.shape
-    first_far = near_mats.shape[0]
+    near = near_mats.shape[0]
     group_batches = group_ref.shape[1]
     far_batches = far_ref.shape[1]
-    first_group = first_far - group_batches
     group_slots = group_out.shape[0]
     far_slots = far_out.shape[0] // 4
     small = [
@@ -121,7 +119,8 @@
     ]
     for copy in small:
         copy.start()
-    chunks = [(at, min(CHUNK, coeffs - at)) for at in range(0, coeffs, CHUNK)]
+    starts = [at for at in CHUNKS if at < coeffs] + [coeffs]
+    chunks = [(at, end - at) for at, end in zip(starts, starts[1:])]
     copies = [
         pltpu.make_async_copy(
             ops_hbm.at[pl.ds(at, size)], ops_buf.at[pl.ds(at, size)], in_sems.at[i]
@@ -155,8 +154,8 @@
             counts.append(dot_nt(hot_u, hot_t).astype(BF))
         return dot_nt(jnp.concatenate(counts, axis=0), flipped)
 
-    far_sum = gathered(far_ref, far_batches, first_far, far_slots)
-    group_sum = gathered(group_ref, group_batches, first_group, group_slots)
+    far_sum = gathered(far_ref, far_batches, near + group_batches, far_slots)
+    group_sum = gathered(group_ref, group_batches, near, group_slots)
     far_own = jnp.transpose(dot_nn(own_half, one_hot(far_send_ref[...], cells)))
     row = scalar_row(lambda i: group_send[0, me[0], i // 8, i % 8], group_slots)
     group_own = jnp.transpose(dot_nn(own_half, one_hot(row, cells)))[:group_slots]
@@ -169,13 +168,17 @@
 
     def take_out(c):
         at = chunks[c][0]
-        size = min(CHUNK, PAD_ROWS - at)
+        size = (chunks[c + 1][0] if c + 1 < len(chunks) else PAD_ROWS) - at
         for i in range(batches):
             low = low_table[pl.ds(at * PITCH + i, size, stride=PITCH), :]
             high = high_table[pl.ds(at * PITCH + i, size, stride=PITCH), :]
-            mats, place = (near_mats, i) if i < first_far else (far_mats, i - first_far)
+            mats, place = (near_mats, i) if i < near else (rest_mats, i - near)
             mats[place, at : at + size, :] = jnp.concatenate([low, high], axis=1).astype(BF)
-        for k, (mats, target) in enumerate(((near_mats, near_ops), (far_mats, far_ops))):
+
+    def send_out(c):
+        at = chunks[c][0]
+        size = (chunks[c + 1][0] if c + 1 < len(chunks) else PAD_ROWS) - at
+        for k, (mats, target) in enumerate(((near_mats, near_ops), (rest_mats, rest_ops))):
             out = pltpu.make_async_copy(
                 mats.at[:, pl.ds(at, size), :],
                 target.at[:, pl.ds(at, size), :],
@@ -195,28 +198,30 @@
                 keep(i, dot_nt(hot[:batches, :LANES], ops_buf[i]))
         if c > 0:
             take_out(c - 1)
+            send_out(c - 1)
     take_out(len(chunks) - 1)
 
     signs = lane_signs()
 
-    def back_terms(summed, mats, count_batches, first, slots):
+    def back_terms(summed, count_batches, first, slots):
         total = jnp.zeros((slots, PAD_ROWS), F32)
         for b in range(count_batches):
             high, low = split(summed[b * slots : (b + 1) * slots])
-            both = dot_nt(jnp.concatenate([high, low], axis=0), mats[first + b])
+            both = dot_nt(jnp.concatenate([high, low], axis=0), rest_mats[first + b])
             total = total + both[:slots] + both[slots:]
         total = total * signs[:, :PAD_ROWS]
         total = jnp.concatenate([total, jnp.zeros((slots, WIDE - PAD_ROWS), F32)], axis=1)
         high, low = split(total)
         return high.astype(F32), low.astype(F32)
 
-    tiles = pack_tiles(*back_terms(far_sum, far_mats, far_batches, 0, far_slots), far_own)
+    far_pair = back_terms(far_sum, far_batches, group_batches, far_slots)
+    group_pair = back_terms(group_sum, group_batches, 0, group_slots)
+    send_out(len(chunks) - 1)
+    tiles = pack_tiles(*far_pair, far_own)
     for i in range(4):
         stage[pl.ds(i, far_slots, stride=4), :] = tiles[i]
     far_out[...] = stage[...].astype(BF)
-    tiles = pack_tiles(
-        *back_terms(group_sum, near_mats, group_batches, first_group, group_slots), group_own
-    )
+    tiles = pack_tiles(*group_pair, group_own)
     group_out[...] = jnp.concatenate(tiles, axis=1).astype(BF)
     for out in outs:
         out.wait()
@@ -233,71 +238,58 @@
 
 
 def near_kernel(
-    me, batch_count, group_send, own_ref, near_ref, group_ref, far_ref, group_in, ops_hbm,
-    out_ref, counts_ref, ops_ref, sems,
+    batch_count, own_ref, near_ref, group_ref, far_ref, ops_ref, out_ref, counts_ref
 ):
-    coeffs, cells = own_ref.shape
-    near = near_ref.shape[1]
-    group_slots = group_in.shape[0]
-    parts = sems.shape[0]
-    size = ops_hbm.shape[0] // parts
-    copies = [
-        pltpu.make_async_copy(
-            ops_hbm.at[pl.ds(i * size, size)], ops_ref.at[pl.ds(i * size, size)], sems.at[i]
-        )
-        for i in range(parts)
-    ]
-    for copy in copies:
-        copy.start()
+    cells = own_ref.shape[1]
+    near = ops_ref.shape[0]
     own_half, flipped = own_tables(own_ref[...])
-    forward, backward, remote = [], [], []
+    forward, backward = [], []
     for b in range(near):
         hot_t, hot_u = pair_hots(near_ref, b, batch_count[0, b], cells, cells)
         forward.append(dot_nt(hot_t, hot_u).astype(BF))
         backward.append(dot_nt(hot_u, hot_t).astype(BF))
     ahead = dot_nt(jnp.concatenate(forward, axis=0), own_half)
     behind = dot_nt(jnp.concatenate(backward, axis=0), flipped)
-    done = near
-    for b in range(group_ref.shape[1]):
-        hot_t, hot_u = pair_hots(group_ref, b, batch_count[0, done], cells, group_slots)
-        remote.append(dot_nt(hot_t, hot_u).astype(BF))
-        done += 1
-    for b in range(far_ref.shape[1]):
-        hot_t, hot_u = pair_hots(far_ref, b, batch_count[0, done], cells, LANES)
-        counts_ref[b] = dot_nt(hot_t, hot_u).astype(BF)
-        done += 1
     total = jnp.zeros((cells, PAD_ROWS), F32)
     mirrored = jnp.zeros((cells, PAD_ROWS), F32)
     for b in range(near):
-        if b % size == 0:
-            copies[b // size].wait()
         part = slice(b * cells, (b + 1) * cells)
         both = dot_nt(
             jnp.concatenate([*split(ahead[part]), *split(behind[part])], axis=0), ops_ref[b]
         )
         total = total + both[:cells] + both[cells : 2 * cells]
         mirrored = mirrored + both[2 * cells : 3 * cells] + both[3 * cells :]
-    total = total + mirrored * lane_signs()[:, :PAD_ROWS]
-    for copy in copies[-(-near // size) :]:
-        copy.wait()
-    tiles = [group_in[:, i * LANES : (i + 1) * LANES].astype(F32) for i in range(4)]
-    high, low, arrived = unpack_tiles(tiles, coeffs)
-    total = forward_terms(total, remote, arrived, lambda b: ops_ref[near + b])
-    row = scalar_row(lambda i: group_send[0, me[0], i // 8, i % 8], group_slots)
-    hot = one_hot(row, cells)[:, :group_slots]
-    out_ref[...] = total + (dot_nn(hot, high) + dot_nn(hot, low))[:, :PAD_ROWS]
-
-
-def finish_kernel(near_sum, counts_ref, ops_ref, far_send_ref, far_in, out_ref, stage):
+    out_ref[...] = total + mirrored * lane_signs()[:, :PAD_ROWS]
+    done = near
+    for pairs_ref in (group_ref, far_ref):
+        for b in range(pairs_ref.shape[1]):
+            hot_t, hot_u = pair_hots(pairs_ref, b, batch_count[0, done], cells, LANES)
+            counts_ref[done - near] = dot_nt(hot_t, hot_u).astype(BF)
+            done += 1
+
+
+def finish_kernel(
+    me, group_send, near_sum, counts_ref, ops_ref, far_send_ref, far_in, group_in, out_ref, stage
+):
     coeffs, cells = out_ref.shape
     far_slots = far_in.shape[0] // 4
+    group_slots = group_in.shape[0]
+    group_batches = counts_ref.shape[0] // 2
     stage[...] = far_in[...].astype(F32)
     tiles = [stage[pl.ds(i, far_slots, stride=4), :] for i in range(4)]
-    high, low, arrived = unpack_tiles(tiles, coeffs)
-    counts = [counts_ref[b] for b in range(counts_ref.shape[0])]
-    total = forward_terms(near_sum[...], counts, arrived, lambda b: ops_ref[b])
-    hot = one_hot(far_send_ref[...], cells)
-    total = total + (dot_nn(hot, high) + dot_nn(hot, low))[:, :PAD_ROWS]
+    far_high, far_low, far_arrived = unpack_tiles(tiles, coeffs)
+    tiles = [group_in[:, i * LANES : (i + 1) * LANES].astype(F32) for i in range(4)]
+    group_high, group_low, group_arrived = unpack_tiles(tiles, coeffs)
+    total = near_sum[...]
+    for first, arrived in ((0, group_arrived), (group_batches, far_arrived)):
+        counts = [counts_ref[first + b][:, : arrived.shape[0]] for b in range(group_batches)]
+        total = forward_terms(total, counts, arrived, lambda b, first=first: ops_ref[first + b])
+    far_hot = one_hot(far_send_ref[...], cells)
+    row = scalar_row(lambda i: group_send[0, me[0], i // 8, i % 8], group_slots)
+    group_hot = one_hot(row, cells)[:, :group_slots]
+    home = dot_nn(far_hot, far_high) + dot_nn(far_hot, far_low)
+    home = home + dot_nn(group_hot, group_high) + dot_nn(group_hot, group_low)
+    total = total + home[:, :PAD_ROWS]
     total = jnp.concatenate([total, jnp.zeros((cells, WIDE - PAD_ROWS), F32)], axis=1)
     out_ref[...] = jnp.transpose(total)[:coeffs]
 
@@ -308,8 +300,8 @@
 ):
     coeffs, cells = multipoles.shape
     batches = batch_class.shape[1]
-    far_batches = far_pairs.shape[1]
-    first_far = batches - far_batches
+    near = local_pairs.shape[1]
+    rest = batches - near
     group_size = lax.axis_size("grp")
     ranges = lax.axis_size("cells")
     far_slots = far_send.shape[1] * far_send.shape[2]
@@ -319,16 +311,16 @@
     smem = pl.BlockSpec(memory_space=pltpu.SMEM)
     vmem = pl.BlockSpec(memory_space=pltpu.VMEM)
     hbm = pl.BlockSpec(memory_space=pl.ANY)
-    chunk_count = -(-coeffs // CHUNK)
-    far_rows, group_rows, ops_near, ops_far = pl.pallas_call(
+    chunk_count = len(CHUNKS)
+    far_rows, group_rows, ops_near, ops_rest = pl.pallas_call(
         prepare_kernel,
         in_specs=[smem] + [hbm] * 8,
         out_specs=[vmem, vmem, hbm, hbm],
         out_shape=[
             jax.ShapeDtypeStruct((far_slots * 4, LANES), BF),
             jax.ShapeDtypeStruct((group_slots, 4 * LANES), BF),
-            jax.ShapeDtypeStruct((first_far, PAD_ROWS, WIDE), BF),
-            jax.ShapeDtypeStruct((far_batches, PAD_ROWS, WIDE), BF),
+            jax.ShapeDtypeStruct((near, PAD_ROWS, WIDE), BF),
+            jax.ShapeDtypeStruct((rest, PAD_ROWS, WIDE), BF),
         ],
         scratch_shapes=[
             pltpu.SMEM(batch_class.shape, jnp.int32),
@@ -341,8 +333,8 @@
             pltpu.VMEM(operators.shape, BF),
             pltpu.VMEM((PAD_ROWS * PITCH, LANES), F32),
             pltpu.VMEM((PAD_ROWS * PITCH, LANES), F32),
-            pltpu.VMEM((first_far, PAD_ROWS, WIDE), BF),
-            pltpu.VMEM((far_batches, PAD_ROWS, WIDE), BF),
+            pltpu.VMEM((near, PAD_ROWS, WIDE), BF),
+            pltpu.VMEM((rest, PAD_ROWS, WIDE), BF),
             pltpu.VMEM((far_slots * 4, LANES), F32),
             pltpu.SemaphoreType.DMA((7,)),
             pltpu.SemaphoreType.DMA((chunk_count,)),
@@ -357,39 +349,33 @@
     group_got = lax.all_to_all(
         group_rows.reshape(group_size, -1, 4 * LANES), "grp", split_axis=0, concat_axis=0, tiled=True
     ).reshape(group_rows.shape)
-    far_got = lax.all_to_all(
-        far_rows.reshape(ranges, -1, LANES), "cells", split_axis=0, concat_axis=0, tiled=True
-    ).reshape(far_rows.shape)
     near_sum, counts = pl.pallas_call(
         near_kernel,
-        in_specs=[smem] * 3 + [vmem] * 5 + [hbm],
+        in_specs=[smem] + [vmem] * 5,
         out_specs=[vmem, vmem],
         out_shape=[
             jax.ShapeDtypeStruct((cells, PAD_ROWS), F32),
-            jax.ShapeDtypeStruct((far_batches, cells, LANES), BF),
+            jax.ShapeDtypeStruct((rest, cells, LANES), BF),
         ],
-        scratch_shapes=[
-            pltpu.VMEM((first_far, PAD_ROWS, WIDE), BF),
-            pltpu.SemaphoreType.DMA((3,)),
-        ],
-        compiler_params=pltpu.CompilerParams(vmem_limit_bytes=NEAR_LIMIT),
+        compiler_params=pltpu.CompilerParams(vmem_limit_bytes=24 * MIB),
         cost_estimate=pl.CostEstimate(
             flops=20_000_000_000, bytes_accessed=40_000_000, transcendentals=0
         ),
         name="near",
-    )(
-        me, batch_count, group_send, multipoles, local_pairs, group_pairs, far_pairs, group_got,
-        ops_near,
-    )
+    )(batch_count, multipoles, local_pairs, group_pairs, far_pairs, ops_near)
+    far_rows, near_sum = lax.optimization_barrier((far_rows, near_sum))
+    far_got = lax.all_to_all(
+        far_rows.reshape(ranges, -1, LANES), "cells", split_axis=0, concat_axis=0, tiled=True
+    ).reshape(far_rows.shape)
     return pl.pallas_call(
         finish_kernel,
-        in_specs=[vmem] * 5,
+        in_specs=[smem] * 2 + [vmem] * 6,
         out_specs=vmem,
         out_shape=jax.ShapeDtypeStruct((coeffs, cells), F32),
         scratch_shapes=[pltpu.VMEM((far_slots * 4, LANES), F32)],
         compiler_params=pltpu.CompilerParams(vmem_limit_bytes=24 * MIB),
         name="finish",
-    )(near_sum, counts, ops_far, far_send, far_got)
+    )(me, group_send, near_sum, counts, ops_rest, far_send, far_got, group_got)
 
 
 def solution(mesh):

time: 63.6 us -> 64.6 us (1.016)
  blocking collectives: 15.3 us -> 37.6 us
  starting transfers between devices: 25 us -> 8.12 us
  Pallas kernels: 17.3 us -> 15.3 us
  waiting for transfers between devices: 3.86 us -> 1.87 us
    all_to_all x1, blocking collectives: 15.3 us -> 37.6 us  [body(): lax.all_to_all(far_rows.reshape(ranges, -1, LANES), 'cells', split_axis=0...]
    all_to_all x1, starting transfers between devices: 25 us -> 8.12 us  [body(): lax.all_to_all(group_rows.reshape(group_size, -1, 4 * LANES), 'grp', spli...]
    all_to_all x1, waiting for transfers between devices: 3.86 us -> 1.87 us  [body(): lax.all_to_all(group_rows.reshape(group_size, -1, 4 * LANES), 'grp', spli...]
    pallas_call x2, Pallas kernels: 8.71 us -> 7.37 us  [the longest x1 3.93 us: body(): pl.pallas_call(near_kernel, in_specs=[smem] + [vmem] * 5, out_specs=[vmem...]
    pallas_call x1, Pallas kernels: 8.58 us -> 7.93 us  [body(): pl.pallas_call(prepare_kernel, in_specs=[smem] + [hbm] * 8, out_specs=[vm...]
    unnamed x18 -> x20, local copies, waits for them, and re-layouts: 1.63 us -> 1.39 us
  transfers between devices with their start and end apart: 1 -> 1, of which waited for: 1 -> 1; matrix products, arithmetic and copies ran while one was open for 0% -> 0% of each run, Pallas kernels for 11% -> 6%
where the time goes in v4:
time: 64.6 us; the launch traced here: 64.3 us
  blocking collectives  37.6 us (58%)
  Pallas kernels  15.3 us (24%)
  starting transfers between devices  8.12 us (13%)
  waiting for transfers between devices  1.87 us (3%)
  local copies, waits for them, and re-layouts  1.39 us (2%)
    all_to_all x1, blocking collectives, body(): lax.all_to_all(far_rows.reshape(ranges, -1, LANES), 'cells', split_axis=0...  37.6 us
    all_to_all x1, starting transfers between devices, body(): lax.all_to_all(group_rows.reshape(group_size, -1, 4 * LANES), 'grp', spli...  8.12 us
    pallas_call x1, Pallas kernels, body(): pl.pallas_call(prepare_kernel, in_specs=[smem] + [hbm] * 8, out_specs=[vm...  7.93 us
    pallas_call x1, Pallas kernels, body(): pl.pallas_call(near_kernel, in_specs=[smem] + [vmem] * 5, out_specs=[vmem...  3.93 us
    pallas_call x1, Pallas kernels, body(): pl.pallas_call(finish_kernel, in_specs=[smem] * 2 + [vmem] * 6, out_specs...  3.44 us
    all_to_all x1, waiting for transfers between devices, body(): lax.all_to_all(group_rows.reshape(group_size, -1, 4 * LANES), 'grp', spli...  1.87 us
    unnamed x20, local copies, waits for them, and re-layouts  1.39 us
  transfers between devices with their start and end apart: 1, of which 1 were waited for; matrix products, arithmetic and copies ran while one was open for 0% of the time, Pallas kernels for 6%

profile of v4, /device:TPU:1, one launch (start us, length us, event | category | flops | bytes accessed | tf_op | source)
XLA Modules:
  0.0 64.3 jit_solution(7775756145711477756)
XLA Ops:
  0.0 0.0 copy-start.2
  0.0 0.0 copy-start.3
  0.0 0.0 copy-start.4
  0.0 0.0 copy-start.6
  0.0 0.0 copy-start.8
  0.0 7.9 %prepare.1 = (bf16[512,128]{1,0:T(8,128)(2,1)}, bf16[64,512]{1,0:T(8,128)(2,1)}, bf16[16,176,256]{2,1,0:T(8,128)(2,1)}, bf16[16,176,256]{2,1,0:T(8,128)(2,1)}) custom-call(s32[1]{0:T(128)} %bitcast.me, s32[1,32]{1,0:T(1,128)} %class_hbm.1, s32[1,32]{1,0:T(1,128)} %batch_count.1, s32[1,8,8,8]{3,2,1,0:T(8,128)} %group_send.1, bf16[165,128]{1,0:T(8,128)(2,1)} %own_ref.1, ...), custom_call_target="tpu_custom_call" | custom-call | tf_op jit(solution)/shard_map/prepare/pallas_call | solution.py:315
  8.0 8.1 %all-to-all-start.1 = ((bf16[8,8,512]{2,1,0:T(8,128)(2,1)}), bf16[8,8,512]{2,1,0:T(8,128)(2,1)S(1)}, u32[]{:S(2)}, u32[]{:S(2)}) async-start(bf16[8,8,512]{2,1,0:T(8,128)(2,1)} %bitcast.11), calls=%async_computation.1 | async-start | bytes 131072 | tf_op jit(solution)/shard_map/all_to_all | solution.py:349
  16.1 0.0 copy-done.2
  16.1 0.0 copy-done.3
  16.1 0.0 copy-done.4
  16.1 0.0 copy-done.6
  16.1 0.0 copy-done.8
  16.1 0.0 copy-start.7
  16.1 1.4 %copy-done.7 = bf16[16,176,256]{2,1,0:T(8,128)(2,1)S(1)} copy-done((bf16[16,176,256]{2,1,0:T(8,128)(2,1)S(1)}, bf16[16,176,256]{2,1,0:T(8,128)(2,1)}, u32[]{:S(2)}) %copy-start.7) | copy-done | bytes 1441816
  17.5 0.0 copy-start.9
  17.5 0.0 copy-start
  17.5 0.0 copy-start.1
  17.5 0.0 copy-start.5
  17.5 3.9 %near.1 = (f32[128,176]{1,0:T(8,128)S(1)}, bf16[16,128,128]{2,1,0:T(8,128)(2,1)S(1)}) custom-call(s32[1,32]{1,0:T(1,128)S(1)} %copy-done.6, bf16[165,128]{1,0:T(8,128)(2,1)S(1)} %copy-done.2, s32[1,16,2,256]{3,2,1,0:T(2,128)S(1)} %copy-done.8, s32[1,8,2,256]{3,2,1,0:T(2,128)S(1)} %copy-done.3, s32[1,8,2,256]{3,2,1,0:T(2,128)S(1)} %copy-done.4, ...), custom_call_target="tpu_custom_call" | custom-call | flops 20000000000 | bytes 40000000 | tf_op jit(solution)/shard_map/near/pallas_call | solution.py:352
  21.4 1.9 %all-to-all-done.1 = bf16[8,8,512]{2,1,0:T(8,128)(2,1)S(1)} async-done(((bf16[8,8,512]{2,1,0:T(8,128)(2,1)}), bf16[8,8,512]{2,1,0:T(8,128)(2,1)S(1)}, u32[]{:S(2)}, u32[]{:S(2)}) %all-to-all-start.1) | async-done | bytes 65568 | tf_op jit(solution)/shard_map/all_to_all | solution.py:349
  23.3 0.0 copy-done.9
  23.3 37.6 %all_to_all.10 = bf16[128,4,128]{2,1,0:T(4,128)(2,1)S(1)} all-to-all(bf16[128,4,128]{2,1,0:T(4,128)(2,1)S(1)} %bitcast.10), channel_id=1, replica_groups=mesh['cells'=128,'grp'=8] {'cells'}, dimensions={0} | all-to-all | bytes 262144 | tf_op jit(solution)/shard_map/all_to_all | solution.py:367
  60.9 0.0 copy-done
  60.9 0.0 copy-done.1
  60.9 0.0 copy-done.5
  60.9 3.4 %finish.1 = f32[165,128]{1,0:T(8,128)} custom-call(s32[1]{0:T(128)} %bitcast.me, s32[1,8,8,8]{3,2,1,0:T(8,128)S(1)} %copy-done.1, f32[128,176]{1,0:T(8,128)S(1)} %get-tuple-element.16.near_sum, bf16[16,128,128]{2,1,0:T(8,128)(2,1)S(1)} %get-tuple-element.17.counts_ref, bf16[16,176,256]{2,1,0:T(8,128)(2,1)S(1)} %copy-done, s32[1,128]{1,0:T(1,128)S(1)} %bitcast.9, ...), custom_call_target="tpu_custom_call" | custom-call | tf_op jit(solution)/shard_map/finish/pallas_call | solution.py:370
Async XLA Ops:
  0.0 16.1 %copy-start.2 = (bf16[165,128]{1,0:T(8,128)(2,1)S(1)}, bf16[165,128]{1,0:T(8,128)(2,1)}, u32[]{:S(2)}) copy-start(bf16[165,128]{1,0:T(8,128)(2,1)} %own_ref.1) | copy-start | bytes 126724
  0.0 16.1 %copy-start.3 = (s32[1,8,2,256]{3,2,1,0:T(2,128)S(1)}, s32[1,8,2,256]{3,2,1,0:T(2,128)}, u32[]{:S(2)}) copy-start(s32[1,8,2,256]{3,2,1,0:T(2,128)} %group_ref.1) | copy-start | bytes 49156
  0.0 16.1 %copy-start.4 = (s32[1,8,2,256]{3,2,1,0:T(2,128)S(1)}, s32[1,8,2,256]{3,2,1,0:T(2,128)}, u32[]{:S(2)}) copy-start(s32[1,8,2,256]{3,2,1,0:T(2,128)} %far_ref.1) | copy-start | bytes 49156
  0.0 16.1 %copy-start.6 = (s32[1,32]{1,0:T(1,128)S(1)}, s32[1,32]{1,0:T(1,128)}, u32[]{:S(2)}) copy-start(s32[1,32]{1,0:T(1,128)} %batch_count.1) | copy-start | bytes 388
  0.0 16.1 %copy-start.8 = (s32[1,16,2,256]{3,2,1,0:T(2,128)S(1)}, s32[1,16,2,256]{3,2,1,0:T(2,128)}, u32[]{:S(2)}) copy-start(s32[1,16,2,256]{3,2,1,0:T(2,128)} %near_ref.1) | copy-start | bytes 98308
  8.0 15.3 %all-to-all-start.1 = ((bf16[8,8,512]{2,1,0:T(8,128)(2,1)}), bf16[8,8,512]{2,1,0:T(8,128)(2,1)S(1)}, u32[]{:S(2)}, u32[]{:S(2)}) async-start(bf16[8,8,512]{2,1,0:T(8,128)(2,1)} %bitcast.11), calls=%async_computation.1 | async-start | bytes 131072 | tf_op jit(solution)/shard_map/all_to_all | solution.py:349
  16.1 1.4 %copy-start.7 = (bf16[16,176,256]{2,1,0:T(8,128)(2,1)S(1)}, bf16[16,176,256]{2,1,0:T(8,128)(2,1)}, u32[]{:S(2)}) copy-start(bf16[16,176,256]{2,1,0:T(8,128)(2,1)} %get-tuple-element.14.ops_ref) | copy-start | bytes 4325380
  17.5 5.8 %copy-start.9 = (bf16[512,128]{1,0:T(8,128)(2,1)S(1)}, bf16[512,128]{1,0:T(8,128)(2,1)}, u32[]{:S(2)}) copy-start(bf16[512,128]{1,0:T(8,128)(2,1)} %get-tuple-element.19) | copy-start | bytes 393220
  17.5 43.4 %copy-start = (bf16[16,176,256]{2,1,0:T(8,128)(2,1)S(1)}, bf16[16,176,256]{2,1,0:T(8,128)(2,1)}, u32[]{:S(2)}) copy-start(bf16[16,176,256]{2,1,0:T(8,128)(2,1)} %get-tuple-element.18.ops_ref) | copy-start | bytes 4325380
  17.5 43.4 %copy-start.1 = (s32[1,8,8,8]{3,2,1,0:T(8,128)S(1)}, s32[1,8,8,8]{3,2,1,0:T(8,128)}, u32[]{:S(2)}) copy-start(s32[1,8,8,8]{3,2,1,0:T(8,128)} %group_send.1) | copy-start | bytes 6148
  17.5 43.4 %copy-start.5 = (s32[1,128,1]{1,2,0:T(1,128)S(1)}, s32[1,128,1]{1,2,0:T(1,128)}, u32[]{:S(2)}) copy-start(s32[1,128,1]{1,2,0:T(1,128)} %param.17) | copy-start | bytes 1540

commit v5 on v3

--- a/solution.py
+++ b/solution.py
@@ -10,10 +10,9 @@
 WIDE = 256
 PAD_ROWS = 176
 PITCH = 40
-CHUNK = 64
+CHUNKS = (0, 96)
 SHIFT = 40
 MIB = 1024 * 1024
-NEAR_LIMIT = 24 * MIB
 BF = jnp.bfloat16
 F32 = jnp.float32
 
@@ -121,7 +120,8 @@
     ]
     for copy in small:
         copy.start()
-    chunks = [(at, min(CHUNK, coeffs - at)) for at in range(0, coeffs, CHUNK)]
+    starts = [at for at in CHUNKS if at < coeffs] + [coeffs]
+    chunks = [(at, end - at) for at, end in zip(starts, starts[1:])]
     copies = [
         pltpu.make_async_copy(
             ops_hbm.at[pl.ds(at, size)], ops_buf.at[pl.ds(at, size)], in_sems.at[i]
@@ -169,12 +169,16 @@
 
     def take_out(c):
         at = chunks[c][0]
-        size = min(CHUNK, PAD_ROWS - at)
+        size = (chunks[c + 1][0] if c + 1 < len(chunks) else PAD_ROWS) - at
         for i in range(batches):
             low = low_table[pl.ds(at * PITCH + i, size, stride=PITCH), :]
             high = high_table[pl.ds(at * PITCH + i, size, stride=PITCH), :]
             mats, place = (near_mats, i) if i < first_far else (far_mats, i - first_far)
             mats[place, at : at + size, :] = jnp.concatenate([low, high], axis=1).astype(BF)
+
+    def send_out(c):
+        at = chunks[c][0]
+        size = (chunks[c + 1][0] if c + 1 < len(chunks) else PAD_ROWS) - at
         for k, (mats, target) in enumerate(((near_mats, near_ops), (far_mats, far_ops))):
             out = pltpu.make_async_copy(
                 mats.at[:, pl.ds(at, size), :],
@@ -195,6 +199,7 @@
                 keep(i, dot_nt(hot[:batches, :LANES], ops_buf[i]))
         if c > 0:
             take_out(c - 1)
+            send_out(c - 1)
     take_out(len(chunks) - 1)
 
     signs = lane_signs()
@@ -210,13 +215,14 @@
         high, low = split(total)
         return high.astype(F32), low.astype(F32)
 
-    tiles = pack_tiles(*back_terms(far_sum, far_mats, far_batches, 0, far_slots), far_own)
+    far_pair = back_terms(far_sum, far_mats, far_batches, 0, far_slots)
+    group_pair = back_terms(group_sum, near_mats, group_batches, first_group, group_slots)
+    send_out(len(chunks) - 1)
+    tiles = pack_tiles(*far_pair, far_own)
     for i in range(4):
         stage[pl.ds(i, far_slots, stride=4), :] = tiles[i]
     far_out[...] = stage[...].astype(BF)
-    tiles = pack_tiles(
-        *back_terms(group_sum, near_mats, group_batches, first_group, group_slots), group_own
-    )
+    tiles = pack_tiles(*group_pair, group_own)
     group_out[...] = jnp.concatenate(tiles, axis=1).astype(BF)
     for out in outs:
         out.wait()
@@ -232,45 +238,33 @@
     return total
 
 
+def count_kernel(batch_count, near_ref, group_ref, far_ref, near_counts, group_counts, far_counts):
+    near = near_ref.shape[1]
+    cells = near_counts.shape[1]
+    for b in range(near):
+        hot_t, hot_u = pair_hots(near_ref, b, batch_count[0, b], cells, cells)
+        near_counts[b] = dot_nt(hot_t, hot_u).astype(BF)
+        near_counts[near + b] = dot_nt(hot_u, hot_t).astype(BF)
+    done = near
+    for pairs_ref, counts_ref in ((group_ref, group_counts), (far_ref, far_counts)):
+        for b in range(pairs_ref.shape[1]):
+            hot_t, hot_u = pair_hots(pairs_ref, b, batch_count[0, done], cells, LANES)
+            counts_ref[b] = dot_nt(hot_t, hot_u).astype(BF)
+            done += 1
+
+
 def near_kernel(
-    me, batch_count, group_send, own_ref, near_ref, group_ref, far_ref, group_in, ops_hbm,
-    out_ref, counts_ref, ops_ref, sems,
+    me, group_send, own_ref, near_counts, group_counts, group_in, ops_ref, out_ref
 ):
     coeffs, cells = own_ref.shape
-    near = near_ref.shape[1]
+    near = near_counts.shape[0] // 2
     group_slots = group_in.shape[0]
-    parts = sems.shape[0]
-    size = ops_hbm.shape[0] // parts
-    copies = [
-        pltpu.make_async_copy(
-            ops_hbm.at[pl.ds(i * size, size)], ops_ref.at[pl.ds(i * size, size)], sems.at[i]
-        )
-        for i in range(parts)
-    ]
-    for copy in copies:
-        copy.start()
     own_half, flipped = own_tables(own_ref[...])
-    forward, backward, remote = [], [], []
-    for b in range(near):
-        hot_t, hot_u = pair_hots(near_ref, b, batch_count[0, b], cells, cells)
-        forward.append(dot_nt(hot_t, hot_u).astype(BF))
-        backward.append(dot_nt(hot_u, hot_t).astype(BF))
-    ahead = dot_nt(jnp.concatenate(forward, axis=0), own_half)
-    behind = dot_nt(jnp.concatenate(backward, axis=0), flipped)
-    done = near
-    for b in range(group_ref.shape[1]):
-        hot_t, hot_u = pair_hots(group_ref, b, batch_count[0, done], cells, group_slots)
-        remote.append(dot_nt(hot_t, hot_u).astype(BF))
-        done += 1
-    for b in range(far_ref.shape[1]):
-        hot_t, hot_u = pair_hots(far_ref, b, batch_count[0, done], cells, LANES)
-        counts_ref[b] = dot_nt(hot_t, hot_u).astype(BF)
-        done += 1
+    ahead = dot_nt(jnp.concatenate([near_counts[b] for b in range(near)], axis=0), own_half)
+    behind = dot_nt(jnp.concatenate([near_counts[near + b] for b in range(near)], axis=0), flipped)
     total = jnp.zeros((cells, PAD_ROWS), F32)
     mirrored = jnp.zeros((cells, PAD_ROWS), F32)
     for b in range(near):
-        if b % size == 0:
-            copies[b // size].wait()
         part = slice(b * cells, (b + 1) * cells)
         both = dot_nt(
             jnp.concatenate([*split(ahead[part]), *split(behind[part])], axis=0), ops_ref[b]
@@ -278,10 +272,9 @@
         total = total + both[:cells] + both[cells : 2 * cells]
         mirrored = mirrored + both[2 * cells : 3 * cells] + both[3 * cells :]
     total = total + mirrored * lane_signs()[:, :PAD_ROWS]
-    for copy in copies[-(-near // size) :]:
-        copy.wait()
     tiles = [group_in[:, i * LANES : (i + 1) * LANES].astype(F32) for i in range(4)]
     high, low, arrived = unpack_tiles(tiles, coeffs)
+    remote = [group_counts[b][:, :group_slots] for b in range(group_counts.shape[0])]
     total = forward_terms(total, remote, arrived, lambda b: ops_ref[near + b])
     row = scalar_row(lambda i: group_send[0, me[0], i // 8, i % 8], group_slots)
     hot = one_hot(row, cells)[:, :group_slots]
@@ -319,7 +312,7 @@
     smem = pl.BlockSpec(memory_space=pltpu.SMEM)
     vmem = pl.BlockSpec(memory_space=pltpu.VMEM)
     hbm = pl.BlockSpec(memory_space=pl.ANY)
-    chunk_count = -(-coeffs // CHUNK)
+    chunk_count = len(CHUNKS)
     far_rows, group_rows, ops_near, ops_far = pl.pallas_call(
         prepare_kernel,
         in_specs=[smem] + [hbm] * 8,
@@ -357,30 +350,36 @@
     group_got = lax.all_to_all(
         group_rows.reshape(group_size, -1, 4 * LANES), "grp", split_axis=0, concat_axis=0, tiled=True
     ).reshape(group_rows.shape)
+    counts_shape = (cells, LANES)
+    near_counts, group_counts, far_counts = pl.pallas_call(
+        count_kernel,
+        in_specs=[smem] + [vmem] * 3,
+        out_specs=[vmem] * 3,
+        out_shape=[
+            jax.ShapeDtypeStruct((n,) + counts_shape, BF)
+            for n in (2 * local_pairs.shape[1], group_pairs.shape[1], far_batches)
+        ],
+        compiler_params=pltpu.CompilerParams(vmem_limit_bytes=60 * MIB),
+        cost_estimate=pl.CostEstimate(
+            flops=10_000_000_000, bytes_accessed=20_000_000, transcendentals=0
+        ),
+        name="count",
+    )(batch_count, local_pairs, group_pairs, far_pairs)
+    far_rows, near_counts = lax.optimization_barrier((far_rows, near_counts))
     far_got = lax.all_to_all(
         far_rows.reshape(ranges, -1, LANES), "cells", split_axis=0, concat_axis=0, tiled=True
     ).reshape(far_rows.shape)
-    near_sum, counts = pl.pallas_call(
+    near_sum = pl.pallas_call(
         near_kernel,
-        in_specs=[smem] * 3 + [vmem] * 5 + [hbm],
-        out_specs=[vmem, vmem],
-        out_shape=[
-            jax.ShapeDtypeStruct((cells, PAD_ROWS), F32),
-            jax.ShapeDtypeStruct((far_batches, cells, LANES), BF),
-        ],
-        scratch_shapes=[
-            pltpu.VMEM((first_far, PAD_ROWS, WIDE), BF),
-            pltpu.SemaphoreType.DMA((3,)),
-        ],
-        compiler_params=pltpu.CompilerParams(vmem_limit_bytes=NEAR_LIMIT),
+        in_specs=[smem, smem] + [vmem] * 5,
+        out_specs=vmem,
+        out_shape=jax.ShapeDtypeStruct((cells, PAD_ROWS), F32),
+        compiler_params=pltpu.CompilerParams(vmem_limit_bytes=24 * MIB),
         cost_estimate=pl.CostEstimate(
             flops=20_000_000_000, bytes_accessed=40_000_000, transcendentals=0
         ),
         name="near",
-    )(
-        me, batch_count, group_send, multipoles, local_pairs, group_pairs, far_pairs, group_got,
-        ops_near,
-    )
+    )(me, group_send, multipoles, near_counts, group_counts, group_got, ops_near)
     return pl.pallas_call(
         finish_kernel,
         in_specs=[vmem] * 5,
@@ -389,7 +388,7 @@
         scratch_shapes=[pltpu.VMEM((far_slots * 4, LANES), F32)],
         compiler_params=pltpu.CompilerParams(vmem_limit_bytes=24 * MIB),
         name="finish",
-    )(near_sum, counts, ops_far, far_send, far_got)
+    )(near_sum, far_counts, ops_far, far_send, far_got)
 
 
 def solution(mesh):

time: 63.6 us -> 63.1 us (level)
  blocking collectives: 15.3 us -> 0 us
  starting transfers between devices: 25 us -> 33.2 us
  waiting for transfers between devices: 3.86 us -> 10.6 us
    all_to_all x1 -> x0, blocking collectives: 15.3 us -> none  [body(): lax.all_to_all(group_rows.reshape(group_size, -1, 4 * LANES), 'grp', spli...]
    all_to_all x0 -> x1, starting transfers between devices: none -> 8.11 us  [body(): lax.all_to_all(group_rows.reshape(group_size, -1, 4 * LANES), 'grp', spli...]
    all_to_all x0 -> x1, waiting for transfers between devices: none -> 4.2 us  [body(): lax.all_to_all(group_rows.reshape(group_size, -1, 4 * LANES), 'grp', spli...]
    all_to_all x1, waiting for transfers between devices: 3.86 us -> 6.43 us  [body(): lax.all_to_all(far_rows.reshape(ranges, -1, LANES), 'cells', split_axis=0...]
    unnamed x18 -> x16, local copies, waits for them, and re-layouts: 1.63 us -> 2.19 us
    pallas_call x1 -> x2, Pallas kernels: 7.18 us -> 7.08 us  [the longest x1 4.08 us: body(): pl.pallas_call(near_kernel, in_specs=[smem, smem] + [vmem] * 5, out_specs...]
  transfers between devices with their start and end apart: 1 -> 2, of which waited for: 1 -> 2; matrix products, arithmetic and copies ran while one was open for 0% -> 0% of each run, Pallas kernels for 11% -> 11%
where the time goes in v5:
time: 63.1 us; the launch traced here: 62.8 us
  starting transfers between devices  33.2 us (53%)
  Pallas kernels  16.7 us (26%)
  waiting for transfers between devices  10.6 us (17%)
  local copies, waits for them, and re-layouts  2.19 us (3%)
    all_to_all x1, starting transfers between devices, body(): lax.all_to_all(far_rows.reshape(ranges, -1, LANES), 'cells', split_axis=0...  25 us
    all_to_all x1, starting transfers between devices, body(): lax.all_to_all(group_rows.reshape(group_size, -1, 4 * LANES), 'grp', spli...  8.11 us
    pallas_call x1, Pallas kernels, body(): pl.pallas_call(prepare_kernel, in_specs=[smem] + [hbm] * 8, out_specs=[vm...  8.1 us
    all_to_all x1, waiting for transfers between devices, body(): lax.all_to_all(far_rows.reshape(ranges, -1, LANES), 'cells', split_axis=0...  6.43 us
    all_to_all x1, waiting for transfers between devices, body(): lax.all_to_all(group_rows.reshape(group_size, -1, 4 * LANES), 'grp', spli...  4.2 us
    pallas_call x1, Pallas kernels, body(): pl.pallas_call(near_kernel, in_specs=[smem, smem] + [vmem] * 5, out_specs...  4.08 us
    pallas_call x1, Pallas kernels, body(): pl.pallas_call(count_kernel, in_specs=[smem] + [vmem] * 3, out_specs=[vme...  3 us
    unnamed x16, local copies, waits for them, and re-layouts  2.19 us
  transfers between devices with their start and end apart: 2, of which 2 were waited for; matrix products, arithmetic and copies ran while one was open for 0% of the time, Pallas kernels for 11%

profile of v5, /device:TPU:1, one launch (start us, length us, event | category | flops | bytes accessed | tf_op | source)
XLA Modules:
  0.0 62.8 jit_solution(8690855568872282835)
XLA Ops:
  0.0 8.1 %prepare.1 = (bf16[512,128]{1,0:T(8,128)(2,1)}, bf16[64,512]{1,0:T(8,128)(2,1)}, bf16[24,176,256]{2,1,0:T(8,128)(2,1)}, bf16[8,176,256]{2,1,0:T(8,128)(2,1)}) custom-call(s32[1]{0:T(128)} %bitcast.me, s32[1,32]{1,0:T(1,128)} %class_hbm.1, s32[1,32]{1,0:T(1,128)} %batch_count.1, s32[1,8,8,8]{3,2,1,0:T(8,128)} %group_send.1, bf16[165,128]{1,0:T(8,128)(2,1)} %own_ref.1, ...), custom_call_target="tpu_custom_call" | custom-call | tf_op jit(solution)/shard_map/prepare/pallas_call | solution.py:316
  8.1 8.1 %all-to-all-start = ((bf16[8,8,512]{2,1,0:T(8,128)(2,1)}), bf16[8,8,512]{2,1,0:T(8,128)(2,1)S(1)}, u32[]{:S(2)}, u32[]{:S(2)}) async-start(bf16[8,8,512]{2,1,0:T(8,128)(2,1)} %bitcast.10), calls=%async_computation | async-start | bytes 131072 | tf_op jit(solution)/shard_map/all_to_all | solution.py:350
  16.2 0.0 copy-start.2
  16.2 0.0 copy-start.3
  16.2 0.0 copy-start.5
  16.3 3.0 %count.1 = (bf16[32,128,128]{2,1,0:T(8,128)(2,1)}, bf16[8,128,128]{2,1,0:T(8,128)(2,1)}, bf16[8,128,128]{2,1,0:T(8,128)(2,1)}) custom-call(s32[1,32]{1,0:T(1,128)} %batch_count.1, s32[1,16,2,256]{3,2,1,0:T(2,128)} %near_ref.1, s32[1,8,2,256]{3,2,1,0:T(2,128)} %group_ref.1, s32[1,8,2,256]{3,2,1,0:T(2,128)} %far_ref.1), custom_call_target="tpu_custom_call" | custom-call | flops 10000000000 | bytes 20000000 | tf_op jit(solution)/shard_map/count/pallas_call | solution.py:354
  19.3 4.2 %all-to-all-done = bf16[8,8,512]{2,1,0:T(8,128)(2,1)S(1)} async-done(((bf16[8,8,512]{2,1,0:T(8,128)(2,1)}), bf16[8,8,512]{2,1,0:T(8,128)(2,1)S(1)}, u32[]{:S(2)}, u32[]{:S(2)}) %all-to-all-start) | async-done | bytes 65568 | tf_op jit(solution)/shard_map/all_to_all | solution.py:350
  23.5 25.0 %all-to-all-start.1 = ((bf16[128,4,128]{2,1,0:T(4,128)(2,1)}), bf16[128,4,128]{2,1,0:T(4,128)(2,1)S(1)}, u32[]{:S(2)}, u32[]{:S(2)}) async-start(bf16[128,4,128]{2,1,0:T(4,128)(2,1)} %bitcast.4), calls=%async_computation.1 | async-start | bytes 262144 | tf_op jit(solution)/shard_map/all_to_all | solution.py:369
  48.5 0.0 copy-done.2
  48.5 0.0 copy-done.3
  48.5 0.0 copy-done.5
  48.5 0.0 copy-start.6
  48.5 1.2 %copy-done.6 = bf16[32,128,128]{2,1,0:T(8,128)(2,1)S(1)} copy-done((bf16[32,128,128]{2,1,0:T(8,128)(2,1)S(1)}, bf16[32,128,128]{2,1,0:T(8,128)(2,1)}, u32[]{:S(2)}) %copy-start.6) | copy-done | bytes 1048600
  49.8 0.0 copy-start.7
  49.8 0.9 %copy-done.7 = bf16[8,128,128]{2,1,0:T(8,128)(2,1)S(1)} copy-done((bf16[8,128,128]{2,1,0:T(8,128)(2,1)S(1)}, bf16[8,128,128]{2,1,0:T(8,128)(2,1)}, u32[]{:S(2)}) %copy-start.7) | copy-done | bytes 262168
  50.7 0.0 copy-start
  50.7 0.0 copy-start.1
  50.7 0.0 copy-start.4
  50.7 4.1 %near.1.near_sum = f32[128,176]{1,0:T(8,128)S(1)} custom-call(s32[1]{0:T(128)} %bitcast.me, s32[1,8,8,8]{3,2,1,0:T(8,128)S(1)} %copy-done.3, bf16[165,128]{1,0:T(8,128)(2,1)S(1)} %copy-done.2, bf16[32,128,128]{2,1,0:T(8,128)(2,1)S(1)} %copy-done.6, bf16[8,128,128]{2,1,0:T(8,128)(2,1)S(1)} %copy-done.7, bf16[64,512]{1,0:T(8,128)(2,1)S(1)} %bitcast.7, ...), custom_call_target="tpu_custom_call" | custom-call | flops 20000000000 | bytes 40000000 | tf_op jit(solution)/shard_map/near/pallas_call | solution.py:372
  54.8 6.4 %all-to-all-done.1 = bf16[128,4,128]{2,1,0:T(4,128)(2,1)S(1)} async-done(((bf16[128,4,128]{2,1,0:T(4,128)(2,1)}), bf16[128,4,128]{2,1,0:T(4,128)(2,1)S(1)}, u32[]{:S(2)}, u32[]{:S(2)}) %all-to-all-start.1) | async-done | bytes 131104 | tf_op jit(solution)/shard_map/all_to_all | solution.py:369
  61.2 0.0 copy-done
  61.2 0.0 copy-done.1
  61.2 0.0 copy-done.4
  61.3 1.5 %finish.1 = f32[165,128]{1,0:T(8,128)} custom-call(f32[128,176]{1,0:T(8,128)S(1)} %near.1.near_sum, bf16[8,128,128]{2,1,0:T(8,128)(2,1)S(1)} %copy-done.1, bf16[8,176,256]{2,1,0:T(8,128)(2,1)S(1)} %copy-done, s32[1,128]{1,0:T(1,128)S(1)} %bitcast.9, bf16[512,128]{1,0:T(8,128)(2,1)S(1)} %bitcast.6), custom_call_target="tpu_custom_call" | custom-call | tf_op jit(solution)/shard_map/finish/pallas_call | solution.py:383
Async XLA Ops:
  8.1 15.3 %all-to-all-start = ((bf16[8,8,512]{2,1,0:T(8,128)(2,1)}), bf16[8,8,512]{2,1,0:T(8,128)(2,1)S(1)}, u32[]{:S(2)}, u32[]{:S(2)}) async-start(bf16[8,8,512]{2,1,0:T(8,128)(2,1)} %bitcast.10), calls=%async_computation | async-start | bytes 131072 | tf_op jit(solution)/shard_map/all_to_all | solution.py:350
  16.2 32.3 %copy-start.2 = (bf16[165,128]{1,0:T(8,128)(2,1)S(1)}, bf16[165,128]{1,0:T(8,128)(2,1)}, u32[]{:S(2)}) copy-start(bf16[165,128]{1,0:T(8,128)(2,1)} %own_ref.1) | copy-start | bytes 126724
  16.2 32.3 %copy-start.3 = (s32[1,8,8,8]{3,2,1,0:T(8,128)S(1)}, s32[1,8,8,8]{3,2,1,0:T(8,128)}, u32[]{:S(2)}) copy-start(s32[1,8,8,8]{3,2,1,0:T(8,128)} %group_send.1) | copy-start | bytes 6148
  16.2 32.3 %copy-start.5 = (bf16[24,176,256]{2,1,0:T(8,128)(2,1)S(1)}, bf16[24,176,256]{2,1,0:T(8,128)(2,1)}, u32[]{:S(2)}) copy-start(bf16[24,176,256]{2,1,0:T(8,128)(2,1)} %get-tuple-element.19.ops_ref) | copy-start | bytes 6488068
  23.5 37.8 %all-to-all-start.1 = ((bf16[128,4,128]{2,1,0:T(4,128)(2,1)}), bf16[128,4,128]{2,1,0:T(4,128)(2,1)S(1)}, u32[]{:S(2)}, u32[]{:S(2)}) async-start(bf16[128,4,128]{2,1,0:T(4,128)(2,1)} %bitcast.4), calls=%async_computation.1 | async-start | bytes 262144 | tf_op jit(solution)/shard_map/all_to_all | solution.py:369
  48.5 1.2 %copy-start.6 = (bf16[32,128,128]{2,1,0:T(8,128)(2,1)S(1)}, bf16[32,128,128]{2,1,0:T(8,128)(2,1)}, u32[]{:S(2)}) copy-start(bf16[32,128,128]{2,1,0:T(8,128)(2,1)} %get-tuple-element.16.near_counts) | copy-start | bytes 3145732
  49.8 0.9 %copy-start.7 = (bf16[8,128,128]{2,1,0:T(8,128)(2,1)S(1)}, bf16[8,128,128]{2,1,0:T(8,128)(2,1)}, u32[]{:S(2)}) copy-start(bf16[8,128,128]{2,1,0:T(8,128)(2,1)} %get-tuple-element.17.group_counts) | copy-start | bytes 786436
  50.7 10.5 %copy-start = (bf16[8,176,256]{2,1,0:T(8,128)(2,1)S(1)}, bf16[8,176,256]{2,1,0:T(8,128)(2,1)}, u32[]{:S(2)}) copy-start(bf16[8,176,256]{2,1,0:T(8,128)(2,1)} %get-tuple-element.21.ops_ref) | copy-start | bytes 2162692
  50.7 10.5 %copy-start.1 = (bf16[8,128,128]{2,1,0:T(8,128)(2,1)S(1)}, bf16[8,128,128]{2,1,0:T(8,128)(2,1)}, u32[]{:S(2)}) copy-start(bf16[8,128,128]{2,1,0:T(8,128)(2,1)} %get-tuple-element.20.counts_ref) | copy-start | bytes 786436
  50.7 10.5 %copy-start.4 = (s32[1,128,1]{1,2,0:T(1,128)S(1)}, s32[1,128,1]{1,2,0:T(1,128)}, u32[]{:S(2)}) copy-start(s32[1,128,1]{1,2,0:T(1,128)} %param.17) | copy-start | bytes 1540

commit v6 on v3

--- a/solution.py
+++ b/solution.py
@@ -10,7 +10,7 @@
 WIDE = 256
 PAD_ROWS = 176
 PITCH = 40
-CHUNK = 64
+CHUNKS = (0, 96)
 SHIFT = 40
 MIB = 1024 * 1024
 NEAR_LIMIT = 24 * MIB
@@ -91,20 +91,54 @@
     return parts
 
 
+def gathered(batch_count, pairs_ref, first_batch, slots, flipped):
+    counts = []
+    for b in range(pairs_ref.shape[1]):
+        hot_t, hot_u = pair_hots(
+            pairs_ref, b, batch_count[0, first_batch + b], flipped.shape[1], slots
+        )
+        counts.append(dot_nt(hot_u, hot_t).astype(BF))
+    return dot_nt(jnp.concatenate(counts, axis=0), flipped)
+
+
+def back_terms(summed, mats, count_batches, first, slots):
+    total = jnp.zeros((slots, PAD_ROWS), F32)
+    for b in range(count_batches):
+        high, low = split(summed[b * slots : (b + 1) * slots])
+        both = dot_nt(jnp.concatenate([high, low], axis=0), mats[first + b])
+        total = total + both[:slots] + both[slots:]
+    total = total * lane_signs()[:, :PAD_ROWS]
+    total = jnp.concatenate([total, jnp.zeros((slots, WIDE - PAD_ROWS), F32)], axis=1)
+    high, low = split(total)
+    return high.astype(F32), low.astype(F32)
+
+
+def far_kernel(batch_count, own_ref, far_ref, far_send_ref, ops_ref, far_out, stage):
+    cells = own_ref.shape[1]
+    far_batches = far_ref.shape[1]
+    far_slots = far_out.shape[0] // 4
+    own_half, flipped = own_tables(own_ref[...])
+    summed = gathered(
+        batch_count, far_ref, batch_count.shape[1] - far_batches, far_slots, flipped
+    )
+    far_own = jnp.transpose(dot_nn(own_half, one_hot(far_send_ref[...], cells)))
+    tiles = pack_tiles(*back_terms(summed, ops_ref, far_batches, 0, far_slots), far_own)
+    for i in range(4):
+        stage[pl.ds(i, far_slots, stride=4), :] = tiles[i]
+    far_out[...] = stage[...].astype(BF)
+
+
 def prepare_kernel(
-    me, class_hbm, count_hbm, send_hbm, own_hbm, ops_hbm, group_hbm, far_hbm, far_send_hbm,
-    far_out, group_out, near_ops, far_ops, batch_class, batch_count, group_send, own_ref, group_ref,
-    far_ref, far_send_ref, ops_buf, low_table, high_table, near_mats, far_mats, stage, small_sems,
-    in_sems, out_sems,
+    me, class_hbm, count_hbm, send_hbm, own_hbm, ops_hbm, group_hbm, group_out, near_ops, far_ops,
+    batch_class, batch_count, group_send, own_ref, group_ref, ops_buf, low_table, high_table,
+    near_mats, far_mats, small_sems, in_sems, out_sems,
 ):
     batches = batch_class.shape[1]
     coeffs, cells = own_ref.shape
     first_far = near_mats.shape[0]
     group_batches = group_ref.shape[1]
-    far_batches = far_ref.shape[1]
     first_group = first_far - group_batches
     group_slots = group_out.shape[0]
-    far_slots = far_out.shape[0] // 4
     small = [
         pltpu.make_async_copy(source, target, small_sems.at[i])
         for i, (source, target) in enumerate(
@@ -114,14 +148,13 @@
                 (send_hbm, group_send),
                 (own_hbm, own_ref),
                 (group_hbm, group_ref),
-                (far_hbm, far_ref),
-                (far_send_hbm, far_send_ref),
             )
         )
     ]
     for copy in small:
         copy.start()
-    chunks = [(at, min(CHUNK, coeffs - at)) for at in range(0, coeffs, CHUNK)]
+    starts = [at for at in CHUNKS if at < coeffs] + [coeffs]
+    chunks = [(at, end - at) for at, end in zip(starts, starts[1:])]
     copies = [
         pltpu.make_async_copy(
             ops_hbm.at[pl.ds(at, size)], ops_buf.at[pl.ds(at, size)], in_sems.at[i]
@@ -146,18 +179,7 @@
 
     own_half, flipped = own_tables(own_ref[...])
 
-    def gathered(pairs_ref, count_batches, first_batch, slots):
-        counts = []
-        for b in range(count_batches):
-            hot_t, hot_u = pair_hots(
-                pairs_ref, b, batch_count[0, first_batch + b], cells, slots
-            )
-            counts.append(dot_nt(hot_u, hot_t).astype(BF))
-        return dot_nt(jnp.concatenate(counts, axis=0), flipped)
-
-    far_sum = gathered(far_ref, far_batches, first_far, far_slots)
-    group_sum = gathered(group_ref, group_batches, first_group, group_slots)
-    far_own = jnp.transpose(dot_nn(own_half, one_hot(far_send_ref[...], cells)))
+    group_sum = gathered(batch_count, group_ref, first_group, group_slots, flipped)
     row = scalar_row(lambda i: group_send[0, me[0], i // 8, i % 8], group_slots)
     group_own = jnp.transpose(dot_nn(own_half, one_hot(row, cells)))[:group_slots]
 
@@ -169,12 +191,16 @@
 
     def take_out(c):
         at = chunks[c][0]
-        size = min(CHUNK, PAD_ROWS - at)
+        size = (chunks[c + 1][0] if c + 1 < len(chunks) else PAD_ROWS) - at
         for i in range(batches):
             low = low_table[pl.ds(at * PITCH + i, size, stride=PITCH), :]
             high = high_table[pl.ds(at * PITCH + i, size, stride=PITCH), :]
             mats, place = (near_mats, i) if i < first_far else (far_mats, i - first_far)
             mats[place, at : at + size, :] = jnp.concatenate([low, high], axis=1).astype(BF)
+
+    def send_out(c):
+        at = chunks[c][0]
+        size = (chunks[c + 1][0] if c + 1 < len(chunks) else PAD_ROWS) - at
         for k, (mats, target) in enumerate(((near_mats, near_ops), (far_mats, far_ops))):
             out = pltpu.make_async_copy(
                 mats.at[:, pl.ds(at, size), :],
@@ -195,28 +221,12 @@
                 keep(i, dot_nt(hot[:batches, :LANES], ops_buf[i]))
         if c > 0:
             take_out(c - 1)
+            send_out(c - 1)
     take_out(len(chunks) - 1)
 
-    signs = lane_signs()
-
-    def back_terms(summed, mats, count_batches, first, slots):
-        total = jnp.zeros((slots, PAD_ROWS), F32)
-        for b in range(count_batches):
-            high, low = split(summed[b * slots : (b + 1) * slots])
-            both = dot_nt(jnp.concatenate([high, low], axis=0), mats[first + b])
-            total = total + both[:slots] + both[slots:]
-        total = total * signs[:, :PAD_ROWS]
-        total = jnp.concatenate([total, jnp.zeros((slots, WIDE - PAD_ROWS), F32)], axis=1)
-        high, low = split(total)
-        return high.astype(F32), low.astype(F32)
-
-    tiles = pack_tiles(*back_terms(far_sum, far_mats, far_batches, 0, far_slots), far_own)
-    for i in range(4):
-        stage[pl.ds(i, far_slots, stride=4), :] = tiles[i]
-    far_out[...] = stage[...].astype(BF)
-    tiles = pack_tiles(
-        *back_terms(group_sum, near_mats, group_batches, first_group, group_slots), group_own
-    )
+    group_pair = back_terms(group_sum, near_mats, group_batches, first_group, group_slots)
+    send_out(len(chunks) - 1)
+    tiles = pack_tiles(*group_pair, group_own)
     group_out[...] = jnp.concatenate(tiles, axis=1).astype(BF)
     for out in outs:
         out.wait()
@@ -319,13 +329,12 @@
     smem = pl.BlockSpec(memory_space=pltpu.SMEM)
     vmem = pl.BlockSpec(memory_space=pltpu.VMEM)
     hbm = pl.BlockSpec(memory_space=pl.ANY)
-    chunk_count = -(-coeffs // CHUNK)
-    far_rows, group_rows, ops_near, ops_far = pl.pallas_call(
+    chunk_count = len(CHUNKS)
+    group_rows, ops_near, ops_far = pl.pallas_call(
         prepare_kernel,
-        in_specs=[smem] + [hbm] * 8,
-        out_specs=[vmem, vmem, hbm, hbm],
+        in_specs=[smem] + [hbm] * 6,
+        out_specs=[vmem, hbm, hbm],
         out_shape=[
-            jax.ShapeDtypeStruct((far_slots * 4, LANES), BF),
             jax.ShapeDtypeStruct((group_slots, 4 * LANES), BF),
             jax.ShapeDtypeStruct((first_far, PAD_ROWS, WIDE), BF),
             jax.ShapeDtypeStruct((far_batches, PAD_ROWS, WIDE), BF),
@@ -336,24 +345,32 @@
             pltpu.SMEM(group_send.shape, jnp.int32),
             pltpu.VMEM(multipoles.shape, BF),
             pltpu.VMEM(group_pairs.shape, jnp.int32),
-            pltpu.VMEM(far_pairs.shape, jnp.int32),
-            pltpu.VMEM(far_send.shape, jnp.int32),
             pltpu.VMEM(operators.shape, BF),
             pltpu.VMEM((PAD_ROWS * PITCH, LANES), F32),
             pltpu.VMEM((PAD_ROWS * PITCH, LANES), F32),
             pltpu.VMEM((first_far, PAD_ROWS, WIDE), BF),
             pltpu.VMEM((far_batches, PAD_ROWS, WIDE), BF),
-            pltpu.VMEM((far_slots * 4, LANES), F32),
-            pltpu.SemaphoreType.DMA((7,)),
+            pltpu.SemaphoreType.DMA((5,)),
             pltpu.SemaphoreType.DMA((chunk_count,)),
             pltpu.SemaphoreType.DMA((2 * chunk_count,)),
         ],
         compiler_params=pltpu.CompilerParams(vmem_limit_bytes=60 * MIB),
         name="prepare",
     )(
-        me, batch_class, batch_count, group_send, multipoles, operators, group_pairs, far_pairs,
-        far_send,
+        me, batch_class, batch_count, group_send, multipoles, operators, group_pairs,
     )
+    far_rows = pl.pallas_call(
+        far_kernel,
+        in_specs=[smem] + [vmem] * 4,
+        out_specs=vmem,
+        out_shape=jax.ShapeDtypeStruct((far_slots * 4, LANES), BF),
+        scratch_shapes=[pltpu.VMEM((far_slots * 4, LANES), F32)],
+        compiler_params=pltpu.CompilerParams(vmem_limit_bytes=60 * MIB),
+        cost_estimate=pl.CostEstimate(
+            flops=10_000_000_000, bytes_accessed=20_000_000, transcendentals=0
+        ),
+        name="far",
+    )(batch_count, multipoles, far_pairs, far_send, ops_far)
     group_got = lax.all_to_all(
         group_rows.reshape(group_size, -1, 4 * LANES), "grp", split_axis=0, concat_axis=0, tiled=True
     ).reshape(group_rows.shape)

time: 63.6 us -> 62.8 us (0.987)
  blocking collectives: 15.3 us -> 0 us
  starting transfers between devices: 25 us -> 33.2 us
  waiting for transfers between devices: 3.86 us -> 8.17 us
  Pallas kernels: 17.3 us -> 19.4 us
    all_to_all x1 -> x0, blocking collectives: 15.3 us -> none  [body(): lax.all_to_all(group_rows.reshape(group_size, -1, 4 * LANES), 'grp', spli...]
    all_to_all x0 -> x1, starting transfers between devices: none -> 8.12 us  [body(): lax.all_to_all(group_rows.reshape(group_size, -1, 4 * LANES), 'grp', spli...]
    all_to_all x0 -> x1, waiting for transfers between devices: none -> 4.28 us  [body(): lax.all_to_all(group_rows.reshape(group_size, -1, 4 * LANES), 'grp', spli...]
    pallas_call x1 -> x2, Pallas kernels: 8.58 us -> 10.7 us  [the longest x1 7.85 us: body(): pl.pallas_call(prepare_kernel, in_specs=[smem] + [hbm] * 6, out_specs=[vm...]
  transfers between devices with their start and end apart: 1 -> 2, of which waited for: 1 -> 2; matrix products, arithmetic and copies ran while one was open for 0% -> 0% of each run, Pallas kernels for 11% -> 16%
where the time goes in v6:
time: 62.8 us; the launch traced here: 62.5 us
  starting transfers between devices  33.2 us (53%)
  Pallas kernels  19.4 us (31%)
  waiting for transfers between devices  8.17 us (13%)
  local copies, waits for them, and re-layouts  1.65 us (3%)
    all_to_all x1, starting transfers between devices, body(): lax.all_to_all(far_rows.reshape(ranges, -1, LANES), 'cells', split_axis=0...  25 us
    all_to_all x1, starting transfers between devices, body(): lax.all_to_all(group_rows.reshape(group_size, -1, 4 * LANES), 'grp', spli...  8.12 us
    pallas_call x1, Pallas kernels, body(): pl.pallas_call(prepare_kernel, in_specs=[smem] + [hbm] * 6, out_specs=[vm...  7.85 us
    pallas_call x1, Pallas kernels, body(): pl.pallas_call(near_kernel, in_specs=[smem] * 3 + [vmem] * 5 + [hbm], out...  7.19 us
    all_to_all x1, waiting for transfers between devices, body(): lax.all_to_all(group_rows.reshape(group_size, -1, 4 * LANES), 'grp', spli...  4.28 us
    all_to_all x1, waiting for transfers between devices, body(): lax.all_to_all(far_rows.reshape(ranges, -1, LANES), 'cells', split_axis=0...  3.88 us
    pallas_call x1, Pallas kernels, body(): pl.pallas_call(far_kernel, in_specs=[smem] + [vmem] * 4, out_specs=vmem,...  2.88 us
    unnamed x18, local copies, waits for them, and re-layouts  1.65 us
  transfers between devices with their start and end apart: 2, of which 2 were waited for; matrix products, arithmetic and copies ran while one was open for 0% of the time, Pallas kernels for 16%

profile of v6, /device:TPU:1, one launch (start us, length us, event | category | flops | bytes accessed | tf_op | source)
XLA Modules:
  0.0 62.5 jit_solution(9926660119878705305)
XLA Ops:
  0.0 7.8 %prepare.1 = (bf16[64,512]{1,0:T(8,128)(2,1)}, bf16[24,176,256]{2,1,0:T(8,128)(2,1)}, bf16[8,176,256]{2,1,0:T(8,128)(2,1)}) custom-call(s32[1]{0:T(128)} %bitcast.me, s32[1,32]{1,0:T(1,128)} %class_hbm.1, s32[1,32]{1,0:T(1,128)} %batch_count.3, s32[1,8,8,8]{3,2,1,0:T(8,128)} %group_send.1, bf16[165,128]{1,0:T(8,128)(2,1)} %own_ref.3, ...), custom_call_target="tpu_custom_call" | custom-call | tf_op jit(solution)/shard_map/prepare/pallas_call | solution.py:333
  7.9 8.1 %all-to-all-start = ((bf16[8,8,512]{2,1,0:T(8,128)(2,1)}), bf16[8,8,512]{2,1,0:T(8,128)(2,1)S(1)}, u32[]{:S(2)}, u32[]{:S(2)}) async-start(bf16[8,8,512]{2,1,0:T(8,128)(2,1)} %bitcast.11), calls=%async_computation | async-start | bytes 131072 | tf_op jit(solution)/shard_map/all_to_all | solution.py:374
  16.0 0.0 copy-start.1
  16.0 0.0 copy-start.2
  16.0 0.0 copy-start.3
  16.0 0.0 copy-start.5
  16.0 0.0 copy-start.7
  16.0 0.0 copy-start.8
  16.0 2.9 %far.1 = bf16[512,128]{1,0:T(8,128)(2,1)} custom-call(s32[1,32]{1,0:T(1,128)} %batch_count.3, bf16[165,128]{1,0:T(8,128)(2,1)} %own_ref.3, s32[1,8,2,256]{3,2,1,0:T(2,128)} %far_ref.3, s32[1,128]{1,0:T(1,128)} %bitcast.8, bf16[8,176,256]{2,1,0:T(8,128)(2,1)} %get-tuple-element.14.ops_ref), custom_call_target="tpu_custom_call" | custom-call | flops 10000000000 | bytes 20000000 | tf_op jit(solution)/shard_map/far/pallas_call | solution.py:362
  18.9 4.3 %all-to-all-done = bf16[8,8,512]{2,1,0:T(8,128)(2,1)S(1)} async-done(((bf16[8,8,512]{2,1,0:T(8,128)(2,1)}), bf16[8,8,512]{2,1,0:T(8,128)(2,1)S(1)}, u32[]{:S(2)}, u32[]{:S(2)}) %all-to-all-start) | async-done | bytes 65568 | tf_op jit(solution)/shard_map/all_to_all | solution.py:374
  23.2 25.0 %all-to-all-start.1 = ((bf16[128,4,128]{2,1,0:T(4,128)(2,1)}), bf16[128,4,128]{2,1,0:T(4,128)(2,1)S(1)}, u32[]{:S(2)}, u32[]{:S(2)}) async-start(bf16[128,4,128]{2,1,0:T(4,128)(2,1)} %bitcast.10), calls=%async_computation.1 | async-start | bytes 262144 | tf_op jit(solution)/shard_map/all_to_all | solution.py:377
  48.3 0.0 copy-done.1
  48.3 0.0 copy-done.2
  48.3 0.0 copy-done.3
  48.3 0.0 copy-done.5
  48.3 0.0 copy-done.7
  48.3 0.0 copy-done.8
  48.3 0.0 copy-start.6
  48.3 1.6 %copy-done.6 = bf16[24,176,256]{2,1,0:T(8,128)(2,1)S(1)} copy-done((bf16[24,176,256]{2,1,0:T(8,128)(2,1)S(1)}, bf16[24,176,256]{2,1,0:T(8,128)(2,1)}, u32[]{:S(2)}) %copy-start.6) | copy-done | bytes 2162712
  49.9 0.0 copy-start
  49.9 0.0 copy-start.4
  49.9 7.2 %near.1 = (f32[128,176]{1,0:T(8,128)S(1)}, bf16[8,128,128]{2,1,0:T(8,128)(2,1)S(1)}) custom-call(s32[1]{0:T(128)} %bitcast.me, s32[1,32]{1,0:T(1,128)S(1)} %copy-done.5, s32[1,8,8,8]{3,2,1,0:T(8,128)S(1)} %copy-done.2, bf16[165,128]{1,0:T(8,128)(2,1)S(1)} %copy-done.1, s32[1,16,2,256]{3,2,1,0:T(2,128)S(1)} %copy-done.7, s32[1,8,2,256]{3,2,1,0:T(2,128)S(1)} %copy-done.3, ...), custom_call_target="tpu_custom_call" | custom-call | flops 20000000000 | bytes 40000000 | tf_op jit(solution)/shard_map/near/pallas_call | solution.py:380
  57.1 3.9 %all-to-all-done.1 = bf16[128,4,128]{2,1,0:T(4,128)(2,1)S(1)} async-done(((bf16[128,4,128]{2,1,0:T(4,128)(2,1)}), bf16[128,4,128]{2,1,0:T(4,128)(2,1)S(1)}, u32[]{:S(2)}, u32[]{:S(2)}) %all-to-all-start.1) | async-done | bytes 131104 | tf_op jit(solution)/shard_map/all_to_all | solution.py:377
  61.0 0.0 copy-done
  61.0 0.0 copy-done.4
  61.0 1.5 %finish.1 = f32[165,128]{1,0:T(8,128)} custom-call(f32[128,176]{1,0:T(8,128)S(1)} %get-tuple-element.12.near_sum, bf16[8,128,128]{2,1,0:T(8,128)(2,1)S(1)} %get-tuple-element.13.counts_ref, bf16[8,176,256]{2,1,0:T(8,128)(2,1)S(1)} %copy-done, s32[1,128]{1,0:T(1,128)S(1)} %bitcast.9, bf16[512,128]{1,0:T(8,128)(2,1)S(1)} %bitcast.6), custom_call_target="tpu_custom_call" | custom-call | tf_op jit(solution)/shard_map/finish/pallas_call | solution.py:401
Async XLA Ops:
  7.9 15.3 %all-to-all-start = ((bf16[8,8,512]{2,1,0:T(8,128)(2,1)}), bf16[8,8,512]{2,1,0:T(8,128)(2,1)S(1)}, u32[]{:S(2)}, u32[]{:S(2)}) async-start(bf16[8,8,512]{2,1,0:T(8,128)(2,1)} %bitcast.11), calls=%async_computation | async-start | bytes 131072 | tf_op jit(solution)/shard_map/all_to_all | solution.py:374
  16.0 32.3 %copy-start.1 = (bf16[165,128]{1,0:T(8,128)(2,1)S(1)}, bf16[165,128]{1,0:T(8,128)(2,1)}, u32[]{:S(2)}) copy-start(bf16[165,128]{1,0:T(8,128)(2,1)} %own_ref.3) | copy-start | bytes 126724
  16.0 32.3 %copy-start.2 = (s32[1,8,8,8]{3,2,1,0:T(8,128)S(1)}, s32[1,8,8,8]{3,2,1,0:T(8,128)}, u32[]{:S(2)}) copy-start(s32[1,8,8,8]{3,2,1,0:T(8,128)} %group_send.1) | copy-start | bytes 6148
  16.0 32.3 %copy-start.3 = (s32[1,8,2,256]{3,2,1,0:T(2,128)S(1)}, s32[1,8,2,256]{3,2,1,0:T(2,128)}, u32[]{:S(2)}) copy-start(s32[1,8,2,256]{3,2,1,0:T(2,128)} %group_ref.1) | copy-start | bytes 49156
  16.0 32.3 %copy-start.5 = (s32[1,32]{1,0:T(1,128)S(1)}, s32[1,32]{1,0:T(1,128)}, u32[]{:S(2)}) copy-start(s32[1,32]{1,0:T(1,128)} %batch_count.3) | copy-start | bytes 388
  16.0 32.3 %copy-start.7 = (s32[1,16,2,256]{3,2,1,0:T(2,128)S(1)}, s32[1,16,2,256]{3,2,1,0:T(2,128)}, u32[]{:S(2)}) copy-start(s32[1,16,2,256]{3,2,1,0:T(2,128)} %near_ref.1) | copy-start | bytes 98308
  16.0 32.3 %copy-start.8 = (s32[1,8,2,256]{3,2,1,0:T(2,128)S(1)}, s32[1,8,2,256]{3,2,1,0:T(2,128)}, u32[]{:S(2)}) copy-start(s32[1,8,2,256]{3,2,1,0:T(2,128)} %far_ref.3) | copy-start | bytes 49156
  23.2 37.8 %all-to-all-start.1 = ((bf16[128,4,128]{2,1,0:T(4,128)(2,1)}), bf16[128,4,128]{2,1,0:T(4,128)(2,1)S(1)}, u32[]{:S(2)}, u32[]{:S(2)}) async-start(bf16[128,4,128]{2,1,0:T(4,128)(2,1)} %bitcast.10), calls=%async_computation.1 | async-start | bytes 262144 | tf_op jit(solution)/shard_map/all_to_all | solution.py:377
  48.3 1.6 %copy-start.6 = (bf16[24,176,256]{2,1,0:T(8,128)(2,1)S(1)}, bf16[24,176,256]{2,1,0:T(8,128)(2,1)}, u32[]{:S(2)}) copy-start(bf16[24,176,256]{2,1,0:T(8,128)(2,1)} %get-tuple-element.11.ops_hbm) | copy-start | bytes 6488068
  49.9 11.1 %copy-start = (bf16[8,176,256]{2,1,0:T(8,128)(2,1)S(1)}, bf16[8,176,256]{2,1,0:T(8,128)(2,1)}, u32[]{:S(2)}) copy-start(bf16[8,176,256]{2,1,0:T(8,128)(2,1)} %get-tuple-element.14.ops_ref) | copy-start | bytes 2162692
  49.9 11.1 %copy-start.4 = (s32[1,128,1]{1,2,0:T(1,128)S(1)}, s32[1,128,1]{1,2,0:T(1,128)}, u32[]{:S(2)}) copy-start(s32[1,128,1]{1,2,0:T(1,128)} %param.17) | copy-start | bytes 1540
